TPU v7x, 512 devices: a whole 4x4x16 slice. The times are simulated.
512 devices in a mesh: seq: 64 (over x, y, z_hi), tensor: 8 (over z_lo, core).
Axes of the slice: x: 4, y: 4, z: 16 (z_hi: 4, z_lo: 4; z = z_hi * 4 + z_lo), core: 2. Of those that a mesh axis runs over, the one named last changes fastest.
Arguments:
- pre_query: bfloat16 [8192, 4096], P('seq', 'tensor'), may hold values from -185 to 185
- pre_key: bfloat16 [8192, 1024], P('seq', 'tensor'), may hold values from -6.2 to 6.2
- pre_value: bfloat16 [8192, 1024], P('seq', 'tensor'), may hold values from -6 to 6
- prompt_lengths: int32 [4], replicated, may hold values from 1 to 5120, 8192 in all
- out_weight: bfloat16 [4096, 4096], P('tensor', 'seq'), may hold values from -0.09375 to 0.09375
- dec_query: bfloat16 [4, 512, 4096], P(None, 'seq', 'tensor'), may hold values from -185 to 185
- dec_key: bfloat16 [4, 512, 1024], P(None, 'seq', 'tensor'), may hold values from -6 to 6
- dec_value: bfloat16 [4, 512, 1024], P(None, 'seq', 'tensor'), may hold values from -6 to 6
- cache_key: bfloat16 [512, 256, 1024], P('seq', None, 'tensor'), may hold values from -6.2 to 6.2
- cache_value: bfloat16 [512, 256, 1024], P('seq', None, 'tensor'), may hold values from -6 to 6
- cache_lengths: int32 [512], P('seq'), may hold values from 1 to 256, 65536 in all
- row_prompt: int32 [512], P('seq'), may hold values from 0 to 3
Outputs:
- prefill_out: bfloat16 [8192, 4096], P('seq', 'tensor')
- decode_out: bfloat16 [4, 512, 4096], P(None, 'seq', 'tensor')
Inputs may be any that keep to these rules, and one draw needn't show every extreme that they name: `prompt_lengths`: they sum to 8192; the largest is exactly 5120. `cache_lengths`: the largest is exactly 256.
All inputs are finite; a program needn't handle non-finite values. No bound on the sum of `cache_lengths` on one device may be relied on, other than what follows from the above.
Results may differ from a plain program's by a relative error of at most 0.023.
Values may be sent and summed in bfloat16 or wider, within the bound.
No kernel may reach another device: no remote copies, remote signals or barrier semaphores. Data moves between devices by JAX's collectives and lax.ppermute only.
A program may use at most 64 MiB of HBM per device.

v0:
```python
import math

import jax
import jax.numpy as jnp
from jax import lax
from jax.sharding import PartitionSpec as P

HD = 128


masked_score = -1e30
block_width = 512


def doc_index(positions, bounds):
    return jnp.sum((positions[:, None] >= bounds[None, :]).astype(jnp.int32), axis=1)


def update_state(fold_state, queries, key_part, value_part, visible):
    running_top, running_total, running_sum = fold_state
    scores = jnp.einsum("grd,kgd->grk", queries, key_part, preferred_element_type=jnp.float32) * (
        1.0 / math.sqrt(HD)
    )
    scores = jnp.where(visible[None], scores, masked_score)
    new_top = jnp.maximum(running_top, jnp.max(scores, axis=2))
    weights = jnp.where(visible[None], jnp.exp(scores - new_top[:, :, None]), 0.0)
    factor = jnp.exp(running_top - new_top)
    running_total = running_total * factor + jnp.sum(weights, axis=2)
    running_sum = running_sum * factor[:, :, None] + jnp.einsum(
        "grk,kgd->grd", weights.astype(jnp.bfloat16), value_part, preferred_element_type=jnp.float32
    )
    return (new_top, running_total, running_sum)


def fold_piece(fold_state, key_piece, value_piece, visitor):
    length = key_piece.shape[0]

    def sub_block(counter, partial_state):
        offset = counter * block_width
        key_part = lax.dynamic_slice_in_dim(key_piece, offset, block_width, 0)
        value_part = lax.dynamic_slice_in_dim(value_piece, offset, block_width, 0)
        return visitor(partial_state, key_part, value_part, offset)

    return lax.fori_loop(0, length // block_width, sub_block, fold_state)


def local_state(scores, visible, value_piece, pattern):
    scores = jnp.where(visible, scores, masked_score)
    top_score = jnp.max(scores, axis=3)
    weights = jnp.where(visible, jnp.exp(scores - top_score[..., None]), 0.0)
    total_weight = jnp.sum(weights, axis=3)
    weighted = jnp.einsum(
        pattern, weights.astype(jnp.bfloat16), value_piece, preferred_element_type=jnp.float32
    )
    leading = top_score.shape[0]
    return (
        top_score.reshape(leading, -1),
        total_weight.reshape(leading, -1),
        weighted.reshape(leading, -1, HD),
    )


def merge_state(first_state, second_state):
    top_score = jnp.maximum(first_state[0], second_state[0])
    first_factor = jnp.exp(first_state[0] - top_score)
    second_factor = jnp.exp(second_state[0] - top_score)
    total_weight = first_state[1] * first_factor + second_state[1] * second_factor
    weighted = (
        first_state[2] * first_factor[:, :, None] + second_state[2] * second_factor[:, :, None]
    )
    return (top_score, total_weight, weighted)


def body(
    pre_query,
    pre_key,
    pre_value,
    prompt_lengths,
    out_weight,
    dec_query,
    dec_key,
    dec_value,
    cache_key,
    cache_value,
    cache_lengths,
    row_prompt,
):
    local_tokens = pre_query.shape[0]
    query_heads = pre_query.shape[1] // HD
    value_heads = pre_key.shape[1] // HD
    group_size = query_heads // value_heads
    steps_count = dec_query.shape[0]
    local_rows = dec_query.shape[1]
    cache_slots = cache_key.shape[1]
    bounds = jnp.cumsum(prompt_lengths)
    first_token = lax.axis_index("seq") * local_tokens
    prefill_rows = local_tokens * group_size
    prefill_queries = (
        pre_query.reshape(local_tokens, value_heads, group_size, HD)
        .transpose(1, 0, 2, 3)
        .reshape(value_heads, prefill_rows, HD)
    )
    query_pos = first_token + jnp.arange(prefill_rows, dtype=jnp.int32) // group_size
    query_doc = doc_index(query_pos, bounds)

    def prefill_visit(fold_state, key_part, value_part, first_index):
        width_here = key_part.shape[0]
        key_pos = first_index + jnp.arange(width_here, dtype=jnp.int32)
        key_doc = doc_index(key_pos, bounds)
        visible = (key_doc[None, :] == query_doc[:, None]) & (
            key_pos[None, :] <= query_pos[:, None]
        )
        return update_state(
            fold_state,
            prefill_queries,
            key_part.reshape(width_here, value_heads, HD),
            value_part.reshape(width_here, value_heads, HD),
            visible,
        )

    per_row = steps_count * group_size
    decode_rows = local_rows * per_row
    decode_queries = (
        dec_query.reshape(steps_count, local_rows, value_heads, group_size, HD)
        .transpose(2, 1, 0, 3, 4)
        .reshape(value_heads, decode_rows, HD)
    )
    row_doc = jnp.repeat(row_prompt, per_row)

    def decode_visit(fold_state, key_part, value_part, first_index):
        width_here = key_part.shape[0]
        key_doc = doc_index(first_index + jnp.arange(width_here, dtype=jnp.int32), bounds)
        visible = key_doc[None, :] == row_doc[:, None]
        return update_state(
            fold_state,
            decode_queries,
            key_part.reshape(width_here, value_heads, HD),
            value_part.reshape(width_here, value_heads, HD),
            visible,
        )

    def empty_state(count_rows):
        return (
            jnp.full((value_heads, count_rows), masked_score, jnp.float32),
            jnp.zeros((value_heads, count_rows), jnp.float32),
            jnp.zeros((value_heads, count_rows, HD), jnp.float32),
        )

    pieces = (
        lax.all_gather(pre_key, "seq", axis=0, tiled=True),
        lax.all_gather(pre_value, "seq", axis=0, tiled=True),
    )
    prefill_state = fold_piece(empty_state(prefill_rows), pieces[0], pieces[1], prefill_visit)
    pieces = (
        lax.all_gather(pre_key, "seq", axis=0, tiled=True),
        lax.all_gather(pre_value, "seq", axis=0, tiled=True),
    )
    decode_state = fold_piece(empty_state(decode_rows), pieces[0], pieces[1], decode_visit)
    pre_attn = prefill_state[2] / prefill_state[1][:, :, None]
    pre_attn = (
        pre_attn.reshape(value_heads, local_tokens, group_size, HD)
        .transpose(1, 0, 2, 3)
        .reshape(local_tokens, query_heads * HD)
        .astype(jnp.bfloat16)
    )
    row_queries = decode_queries.reshape(value_heads, local_rows, per_row, HD)
    cache_keys = cache_key.reshape(local_rows, cache_slots, value_heads, HD)
    cache_values = cache_value.reshape(local_rows, cache_slots, value_heads, HD)
    cache_scores = jnp.einsum(
        "grqd,rkgd->grqk", row_queries, cache_keys, preferred_element_type=jnp.float32
    ) * (1.0 / math.sqrt(HD))
    cache_seen = (jnp.arange(cache_slots, dtype=jnp.int32)[None, :] < cache_lengths[:, None])[
        None, :, None, :
    ]
    cache_state = local_state(cache_scores, cache_seen, cache_values, "grqk,rkgd->grqd")
    new_keys = dec_key.reshape(steps_count, local_rows, value_heads, HD)
    new_values = dec_value.reshape(steps_count, local_rows, value_heads, HD)
    new_scores = jnp.einsum(
        "grqd,urgd->grqu", row_queries, new_keys, preferred_element_type=jnp.float32
    ) * (1.0 / math.sqrt(HD))
    step_of = jnp.arange(per_row, dtype=jnp.int32) // group_size
    new_seen = (jnp.arange(steps_count, dtype=jnp.int32)[None, :] <= step_of[:, None])[None, None]
    new_state = local_state(new_scores, new_seen, new_values, "grqu,urgd->grqd")
    merged = merge_state(merge_state(decode_state, cache_state), new_state)
    dec_attn = merged[2] / merged[1][:, :, None]
    dec_attn = (
        dec_attn.reshape(value_heads, local_rows, steps_count, group_size, HD)
        .transpose(2, 1, 0, 3, 4)
        .reshape(steps_count * local_rows, query_heads * HD)
        .astype(jnp.bfloat16)
    )
    stacked = jnp.concatenate([pre_attn, dec_attn], axis=0)
    products = jnp.dot(
        stacked,
        lax.all_gather(out_weight, "seq", axis=1, tiled=True),
        preferred_element_type=jnp.float32,
    )
    summed = lax.psum_scatter(
        products.astype(jnp.bfloat16), "tensor", scatter_dimension=1, tiled=True
    )
    prefill_out = summed[:local_tokens]
    decode_out = summed[local_tokens:].reshape(steps_count, local_rows, summed.shape[1])
    return (prefill_out, decode_out)


def solution(mesh):
    placed = (
        P("seq", "tensor"),
        P("seq", "tensor"),
        P("seq", "tensor"),
        P(),
        P("tensor", "seq"),
        P(None, "seq", "tensor"),
        P(None, "seq", "tensor"),
        P(None, "seq", "tensor"),
        P("seq", None, "tensor"),
        P("seq", None, "tensor"),
        P("seq"),
        P("seq"),
    )
    return jax.shard_map(
        body,
        mesh=mesh,
        in_specs=placed,
        out_specs=(P("seq", "tensor"), P(None, "seq", "tensor")),
        check_vma=False,
    )
```

profile of v0, /device:TPU:1, one launch (start us, length us, event | category | flops | bytes accessed | tf_op | source)
XLA Modules:
  0.0 436.7 jit_solution(10017208821049179563)
XLA Ops:
  16.0 114.4 %all-gather.4.cloned.1.call-done = bf16[8192,128]{1,0:T(8,128)(2,1)} async-done(((bf16[128,128]{1,0:T(8,128)(2,1)}), bf16[8192,128]{1,0:T(8,128)(2,1)}) %all-gather.4.cloned.1.call-update) | async-done | bytes 2097168 | tf_op jit(solution)/shard_map/all_gather | solution.py:150
  130.4 113.5 %all-gather.6.cloned.1.call-done = bf16[8192,128]{1,0:T(8,128)(2,1)} async-done(((bf16[128,128]{1,0:T(8,128)(2,1)}), bf16[8192,128]{1,0:T(8,128)(2,1)}) %all-gather.6.cloned.1.call-update) | async-done | bytes 2097168 | tf_op jit(solution)/shard_map/all_gather | solution.py:151
  243.9 52.8 %while.36 = (s32[]{:T(128)}, f32[1,512]{1,0:T(1,128)S(1)}, f32[1,512]{1,0:T(1,128)S(1)}, f32[1,512,128]{2,1,0:T(8,128)S(1)}, s32[4]{0:T(128)S(1)}, /*index=5*/s3...) while((s32[]{:T(128)}, f32[1,512]{1,0:T(1,128)S(1)}, ...), condition=%wide.region_6.7_spmd.clone, body=%wide.region_2.6_spmd.clone.sunk | while | flops 139146240 | bytes 4128991 | solution.py:44
  245.7 1.5 fusion.118
  249.0 1.5 fusion.118
  250.6 1.3 fusion.114
  252.3 1.5 fusion.118
  253.9 1.3 fusion.114
  255.6 1.5 fusion.118
  258.9 1.5 fusion.118
  262.2 1.5 fusion.118
  263.8 1.3 fusion.114
  265.5 1.5 fusion.118
  267.1 1.3 fusion.114
  268.8 1.5 fusion.118
  270.4 1.3 fusion.114
  272.1 1.5 fusion.118
  273.7 1.3 fusion.114
  275.4 1.5 fusion.118
  278.7 1.5 fusion.118
  282.0 1.5 fusion.118
  285.3 1.5 fusion.118
  288.6 1.5 fusion.118
  290.2 1.3 fusion.114
  291.9 1.5 fusion.118
  295.2 1.5 fusion.118
  296.8 46.0 %while.37 = (s32[]{:T(128)}, f32[1,128]{1,0:T(1,128)S(1)}, f32[1,128]{1,0:T(1,128)S(1)}, f32[1,128,128]{2,1,0:T(8,128)S(1)}, s32[4]{0:T(128)S(1)}, /*index=5*/bf...) while((s32[]{:T(128)}, f32[1,128]{1,0:T(1,128)S(1)}, ...), condition=%wide.region_11.12_spmd.clone, body=%wide.region_7.11_spmd.clone.sunk | while | flops 34396936 | bytes 1236211 | solution.py:44
  343.2 41.1 %all-gather.8.cloned.1.call-done = bf16[512,4096]{0,1:T(8,128)(2,1)} async-done(((bf16[512,64]{0,1:T(8,128)(2,1)}), bf16[512,4096]{0,1:T(8,128)(2,1)}) %all-gather.8.cloned.1.call-update) | async-done | bytes 4194320 | tf_op jit(solution)/shard_map/all_gather | solution.py:195
  384.3 4.8 %convolution_convert_fusion = bf16[160,4096]{1,0:T(8,128)(2,1)} fusion(bf16[512,4096]{0,1:T(8,128)(2,1)} %all-gather.8.cloned.1.call-done, bf16[32,512]{1,0:T(8,128)(2,1)S(1)} %bitcast.115, bf16[128,512]{1,0:T(8,128)(2,1)S(1)} %convert_element_type.64), kind=kOutput, calls=%fused_computation.68 | convolution fusion | flops 672071680 | bytes 5668864 | tf_op jit(solution)/shard_map/dot_general | solution.py:193
  389.1 38.2 %reduce-scatter.2.cloned.1.call-done = bf16[160,512]{1,0:T(8,128)(2,1)} async-done(((bf16[160,4096]{1,0:T(8,128)(2,1)}), bf16[160,512]{1,0:T(8,128)(2,1)}) %reduce-scatter.2.cloned.1.call-update) | async-done | bytes 163856 | tf_op jit(solution)/shard_map/reduce_scatter | solution.py:198
  427.2 1.6 slice.8
  428.8 1.4 slice_bitcast_fusion
  (308 shorter events, 72.9 us)
Async XLA Ops:
  7.2 3.9 copy-start
  7.2 8.6 %copy-start.1 = (bf16[128,512]{1,0:T(8,128)(2,1)S(1)}, bf16[128,512]{1,0:T(8,128)(2,1)}, u32[]{:S(2)}) copy-start(bf16[128,512]{1,0:T(8,128)(2,1)} %param.16) | copy-start | bytes 393220
  7.2 123.2 %all-gather.4.cloned.1.call-start = ((), (), s32[]{:S(2)}) async-start(), calls=%async_computation.1 | async-start | bytes 2129920 | tf_op jit(solution)/shard_map/all_gather | solution.py:150
  7.9 236.0 %all-gather.6.cloned.1.call-start = ((), (), s32[]{:S(2)}) async-start(), calls=%async_computation.2 | async-start | bytes 2129920 | tf_op jit(solution)/shard_map/all_gather | solution.py:151
  8.7 375.6 %all-gather.8.cloned.1.call-start = ((), (), s32[]{:S(2)}) async-start(), calls=%async_computation.3 | async-start | bytes 4259840 | tf_op jit(solution)/shard_map/all_gather | solution.py:195
  9.4 417.8 %reduce-scatter.2.cloned.1.call-start = ((), (), s32[]{:S(2)}) async-start(), calls=%async_computation.4 | async-start | bytes 1474560 | tf_op jit(solution)/shard_map/reduce_scatter | solution.py:198
  243.9 52.8 %copy-start.2 = (s32[8]{0:T(128)S(1)}, s32[8]{0:T(128)}, u32[]{:S(2)}) copy-start(s32[8]{0:T(128)} %param.27) | copy-start | bytes 100
Sparse Core Ops, SparseCore 0:
  12.2 118.1 all-gather.3
  134.6 109.2 all-gather.5
  248.1 136.1 all-gather.7
  389.2 37.9 reduce-scatter.1
where the time goes:
time: 440 us; the launch traced here: 437 us
  waiting for transfers between devices  309 us (70%)
  matrix products  91.4 us (21%)
  between operations  13.9 us (3%)
  other arithmetic  13.4 us (3%)
  local copies, waits for them, and re-layouts  6.72 us (2%)
    all_gather x1, waiting for transfers between devices, body(): lax.all_gather(pre_key, 'seq', axis=0, tiled=True)  114 us
    all_gather x1, waiting for transfers between devices, body(): lax.all_gather(pre_value, 'seq', axis=0, tiled=True)  114 us
    dot_general x32, matrix products, update_state(): jnp.einsum('grk,kgd->grd', weights.astype(jnp.bfloat16), value_part, pref...  44.3 us
    all_gather x1, waiting for transfers between devices, body(): lax.all_gather(out_weight, 'seq', axis=1, tiled=True)  41.1 us
    dot_general x32, matrix products, update_state(): jnp.einsum('grd,kgd->grk', queries, key_part, preferred_element_type=jnp....  39.1 us
    reduce_scatter x1, waiting for transfers between devices, body(): lax.psum_scatter(products.astype(jnp.bfloat16), 'tensor', scatter_dimensi...  38.2 us
  transfers between devices with their start and end apart: 4, of which 4 were waited for; matrix products, arithmetic and copies ran while one was open for 24% of the time, Pallas kernels for 0%

commit v1 on v0

v1 whole, which is shorter than its diff:
```python
import functools
import math

import jax
import jax.numpy as jnp
from jax import lax
from jax.experimental import pallas as pl
from jax.experimental.pallas import tpu as pltpu
from jax.sharding import Mesh, PartitionSpec as P

HD = 128
GROUP = 4
STEPS = 4
BLOCK = 512
MASKED = -1e30
SCALE = math.log2(math.e) / math.sqrt(HD)


def fold(state, queries, keys, values, visible):
    top, total, acc = state
    scores = lax.dot_general(
        keys, queries, (((1,), (1,)), ((), ())), preferred_element_type=jnp.float32
    )
    scores = scores * SCALE
    if visible is not None:
        scores = jnp.where(visible, scores, MASKED)
    new_top = jnp.maximum(top, jnp.max(scores, axis=0, keepdims=True))
    weights = jnp.exp2(scores - new_top)
    factor = jnp.exp2(top - new_top)
    total = total * factor + jnp.sum(weights, axis=0, keepdims=True)
    acc = acc * factor + lax.dot_general(
        values,
        weights.astype(jnp.bfloat16),
        (((0,), (0,)), ((), ())),
        preferred_element_type=jnp.float32,
    )
    return new_top, total, acc


def by_head(ref):
    return jnp.concatenate([ref[:, h * HD : (h + 1) * HD] for h in range(GROUP)], axis=0)


def cache_kernel(len_ref, q_ref, nk_ref, nv_ref, ck_ref, cv_ref, top_ref, total_ref, acc_ref):
    rows = len_ref.shape[0]
    slots = ck_ref.shape[0] // rows
    new = nk_ref.shape[0]
    queries = by_head(q_ref)
    lanes = queries.shape[0]
    lane = lax.broadcasted_iota(jnp.int32, (1, lanes), 1)
    lane_row = lax.rem(lane, rows)
    lane_step = lax.rem(lane // rows, STEPS)
    state = (
        jnp.full((1, lanes), MASKED, jnp.float32),
        jnp.zeros((1, lanes), jnp.float32),
        jnp.zeros((HD, lanes), jnp.float32),
    )
    key = lax.broadcasted_iota(jnp.int32, (new, lanes), 0)
    seen = (lax.rem(key, rows) == lane_row) & (key // rows <= lane_step)
    state = fold(state, queries, nk_ref[...], nv_ref[...], seen)
    slot = lax.broadcasted_iota(jnp.int32, (slots, lanes), 0)
    for r in range(rows):
        limit = jnp.where(lane_row == r, len_ref[r], 0)
        state = fold(
            state,
            queries,
            ck_ref[r * slots : (r + 1) * slots, :],
            cv_ref[r * slots : (r + 1) * slots, :],
            slot < limit,
        )
    top_ref[...] = state[0]
    total_ref[...] = state[1]
    acc_ref[...] = state[2]


def prompt_kernel(
    bound_ref, prompt_ref, first_ref, q_ref, dq_ref, kv_ref, top_ref, total_ref, acc_ref, out_ref
):
    prompts = bound_ref.shape[0] - 1
    rows = prompt_ref.shape[0]
    tokens = q_ref.shape[0]
    first = first_ref[0]

    def run(state, queries, low, high, begin, end):
        lanes = queries.shape[0]
        key = lax.broadcasted_iota(jnp.int32, (BLOCK, lanes), 0)

        def step(block, state):
            start = pl.multiple_of(block * BLOCK, BLOCK)
            pos = key + start
            return fold(
                state,
                queries,
                kv_ref[pl.ds(start, BLOCK), :HD],
                kv_ref[pl.ds(start, BLOCK), HD:],
                (pos >= low) & (pos < high),
            )

        state = lax.fori_loop(begin, end, step, state)
        return state[2] / state[1]

    queries = by_head(q_ref)
    lanes = queries.shape[0]
    lane = lax.broadcasted_iota(jnp.int32, (1, lanes), 1)
    pos = first + lax.rem(lane, tokens)
    low = jnp.zeros((1, lanes), jnp.int32)
    first_low = jnp.int32(0)
    for b in range(1, prompts):
        low = jnp.where(pos >= bound_ref[b], bound_ref[b], low)
        first_low = jnp.where(first >= bound_ref[b], bound_ref[b], first_low)
    state = (
        jnp.full((1, lanes), MASKED, jnp.float32),
        jnp.zeros((1, lanes), jnp.float32),
        jnp.zeros((HD, lanes), jnp.float32),
    )
    done = run(
        state, queries, low, pos + 1, first_low // BLOCK, (first + tokens - 1) // BLOCK + 1
    )
    for h in range(GROUP):
        out_ref[:tokens, h * HD : (h + 1) * HD] = done[:, h * tokens : (h + 1) * tokens].T.astype(
            jnp.bfloat16
        )

    queries = by_head(dq_ref)
    lanes = queries.shape[0]
    lane_row = lax.rem(lax.broadcasted_iota(jnp.int32, (1, lanes), 1), rows)
    low = jnp.zeros((1, lanes), jnp.int32)
    high = jnp.zeros((1, lanes), jnp.int32)
    begin = bound_ref[prompts]
    end = jnp.int32(0)
    for r in range(rows):
        which = prompt_ref[r]
        row_low, row_high = bound_ref[which], bound_ref[which + 1]
        low = jnp.where(lane_row == r, row_low, low)
        high = jnp.where(lane_row == r, row_high, high)
        begin = jnp.minimum(begin, row_low)
        end = jnp.maximum(end, row_high)
    state = (top_ref[...], total_ref[...], acc_ref[...])
    done = run(
        state, queries, low, high, begin // BLOCK, (end + BLOCK - 1) // BLOCK
    ).T.astype(jnp.bfloat16)
    each = lanes // GROUP
    for h in range(GROUP):
        out_ref[tokens:, h * HD : (h + 1) * HD] = done[h * each : (h + 1) * each, :]


def copies(x, count):
    return jnp.broadcast_to(x[None], (count,) + x.shape)


def body(
    pre_query,
    pre_key,
    pre_value,
    prompt_lengths,
    out_weight,
    dec_query,
    dec_key,
    dec_value,
    cache_key,
    cache_value,
    cache_lengths,
    row_prompt,
):
    tokens = pre_query.shape[0]
    steps, rows, width = dec_query.shape
    slots = cache_key.shape[1]
    X, Y, H, L = (lax.axis_size(a) for a in ("x", "y", "zh", "zl"))
    x, y, zh, zl, core = (lax.axis_index(a) for a in ("x", "y", "zh", "zl", "core"))
    smem = pl.BlockSpec(memory_space=pltpu.SMEM)
    vmem = pl.BlockSpec(memory_space=pltpu.VMEM)
    params = pltpu.CompilerParams(vmem_limit_bytes=40 * 2**20)

    with jax.named_scope("gather_weight"):
        weight = lax.all_gather(out_weight.T, ("y", "zh"), axis=0, tiled=True)
    with jax.named_scope("gather_kv"):
        kv = jnp.concatenate([pre_key, pre_value], axis=1)
        kv = lax.all_gather(kv, "zh", axis=0, tiled=True)
        kv = lax.all_to_all(copies(kv, X * Y), ("x", "y"), 0, 0)
        kv = kv.reshape(-1, 2 * HD)

    dq = dec_query.reshape(steps * rows, width)
    lanes = steps * rows * GROUP
    with jax.named_scope("cache"):
        state = pl.pallas_call(
            cache_kernel,
            out_shape=(
                jax.ShapeDtypeStruct((1, lanes), jnp.float32),
                jax.ShapeDtypeStruct((1, lanes), jnp.float32),
                jax.ShapeDtypeStruct((HD, lanes), jnp.float32),
            ),
            in_specs=[smem] + [vmem] * 5,
            out_specs=(vmem, vmem, vmem),
            compiler_params=params,
            cost_estimate=pl.CostEstimate(
                flops=4 * lanes * HD * rows * slots,
                bytes_accessed=4 * rows * slots * HD,
                transcendentals=lanes * rows * slots,
            ),
        )(
            cache_lengths,
            dq,
            dec_key.reshape(steps * rows, HD),
            dec_value.reshape(steps * rows, HD),
            cache_key.reshape(rows * slots, HD),
            cache_value.reshape(rows * slots, HD),
        )

    bounds = jnp.concatenate([jnp.zeros((1,), jnp.int32), jnp.cumsum(prompt_lengths)]).astype(
        jnp.int32
    )
    first = (((x * Y + y) * H + zh) * tokens).astype(jnp.int32).reshape(1)
    with jax.named_scope("attend"):
        attn = pl.pallas_call(
            prompt_kernel,
            out_shape=jax.ShapeDtypeStruct((tokens + steps * rows, width), jnp.bfloat16),
            in_specs=[smem] * 3 + [vmem] * 6,
            out_specs=vmem,
            compiler_params=params,
            cost_estimate=pl.CostEstimate(
                flops=4 * (lanes + tokens * GROUP) * HD * kv.shape[0],
                bytes_accessed=2 * kv.size,
                transcendentals=(lanes + tokens * GROUP) * kv.shape[0],
            ),
        )(bounds, row_prompt, first, pre_query, dq, kv, *state)

    total = attn.shape[0]
    with jax.named_scope("gather_attn"):
        attn = lax.all_to_all(copies(attn, X), "x", 0, 0).reshape(X * total, width)
    with jax.named_scope("project"):
        half = weight.shape[0] // 2

        def product(which):
            part = lax.dynamic_slice_in_dim(weight, which * half, half, 0)
            return lax.dot_general(
                attn, part, (((1,), (1,)), ((), ())), preferred_element_type=jnp.float32
            ).astype(jnp.bfloat16)

        other = lax.ppermute(product(1 - core), "core", [(0, 1), (1, 0)])
        mine = product(core)
        mine = (mine.astype(jnp.float32) + other.astype(jnp.float32)).astype(jnp.bfloat16)
    with jax.named_scope("scatter"):
        pieces = mine.reshape(X, total, half)
        result = None
        for k in range(X):
            to = lax.rem(zl + k, X)
            piece = lax.dynamic_index_in_dim(pieces, to, 0, keepdims=False)
            pairs = [(a * L + b, ((b + k) % X) * L + a) for a in range(X) for b in range(L)]
            piece = lax.ppermute(piece, ("x", "zl"), pairs).astype(jnp.float32)
            result = piece if result is None else result + piece
        result = result.astype(jnp.bfloat16)
    return result[:tokens], result[tokens:].reshape(steps, rows, half)


def solution(mesh):
    fine = Mesh(mesh.devices.reshape(4, 4, 4, 4, 2), ("x", "y", "zh", "zl", "core"))
    seq, tensor = ("x", "y", "zh"), ("zl", "core")
    placed = (
        P(seq, tensor),
        P(seq, tensor),
        P(seq, tensor),
        P(),
        P(tensor, seq),
        P(None, seq, tensor),
        P(None, seq, tensor),
        P(None, seq, tensor),
        P(seq, None, tensor),
        P(seq, None, tensor),
        P(seq),
        P(seq),
    )
    return jax.shard_map(
        body,
        mesh=fine,
        in_specs=placed,
        out_specs=(P(seq, tensor), P(None, seq, tensor)),
        check_vma=False,
    )
```

time: 440 us -> 202 us (0.46)
  the two profiles are of different devices: /device:TPU:1 before, /device:TPU:10 now
where the time goes in v1:
time: 202 us
  waiting for transfers between devices  108 us (53%)
  starting transfers between devices  32.3 us (16%)
  blocking collectives  26.9 us (13%)
  between operations  14.2 us (7%)
  Pallas kernels  12.6 us (6%)
  local copies, waits for them, and re-layouts  4.7 us (2%)
  matrix products  2.2 us (1%)
    all_to_all x1, waiting for transfers between devices, body(): kv = lax.all_to_all(copies(kv, X * Y), ('x', 'y'), 0, 0)  45.5 us
    ppermute x4, waiting for transfers between devices, body(): piece = lax.ppermute(piece, ('x', 'zl'), pairs).astype(jnp.float32)  34.3 us
    all_gather x1, blocking collectives, body(): kv = lax.all_gather(kv, 'zh', axis=0, tiled=True)  26.9 us
    all_gather x1, waiting for transfers between devices, body(): weight = lax.all_gather(out_weight.T, ('y', 'zh'), axis=0, tiled=True)  25.4 us
    ppermute x4, starting transfers between devices, body(): piece = lax.ppermute(piece, ('x', 'zl'), pairs).astype(jnp.float32)  12.4 us
    pallas_call x1, Pallas kernels, body(): pl.pallas_call(prompt_kernel, out_shape=jax.ShapeDtypeStruct((tokens + st...  11.2 us
    all_to_all x1, starting transfers between devices, body(): attn = lax.all_to_all(copies(attn, X), 'x', 0, 0).reshape(X * total, width)  10.4 us
    all_to_all x1, starting transfers between devices, body(): kv = lax.all_to_all(copies(kv, X * Y), ('x', 'y'), 0, 0)  7.51 us
  transfers between devices with their start and end apart: 8, of which 5 were waited for; matrix products, arithmetic and copies ran while one was open for 1% of the time, Pallas kernels for 6%

profile of v1, /device:TPU:10, one launch (start us, length us, event | category | flops | bytes accessed | tf_op | source)
XLA Modules:
  0.0 202.0 jit_solution(6491432058589570006)
XLA Ops:
  7.2 0.8 pad_maximum_fusion
  7.9 26.9 %all_gather.6 = bf16[512,256]{1,0:T(8,128)(2,1)S(1)} all-gather(bf16[128,256]{1,0:T(8,128)(2,1)S(1)} %pad_maximum_fusion), channel_id=1, replica_groups=mesh['x'=4,'y'=4,'zh'=4,'zl'=4,'core'=2] {'zh'}, dimensions={0}, use_global_device_ids=true | all-gather | bytes 327680 | tf_op jit(solution)/shard_map/gather_kv/all_gather | solution.py:178
  34.8 2.4 %broadcast_in_dim.4 = bf16[16,512,256]{2,1,0:T(8,128)(2,1)} broadcast(bf16[512,256]{1,0:T(8,128)(2,1)S(1)} %all_gather.6), dimensions={1,2} | broadcast | bytes 4456448 | tf_op jit(solution)/shard_map/gather_kv/broadcast_in_dim | solution.py:148
  37.3 0.0 copy-start.3
  37.3 0.0 copy-start.4
  37.3 0.0 copy-start.6
  37.3 0.0 copy-start.7
  37.3 7.5 %all-to-all-start = ((bf16[16,512,256]{2,1,0:T(8,128)(2,1)}), bf16[16,512,256]{2,1,0:T(8,128)(2,1)}, u32[]{:S(2)}, u32[]{:S(2)}) async-start(bf16[16,512,256]{2,1,0:T(8,128)(2,1)} %broadcast_in_dim.4), calls=%async_computation | async-start | bytes 8388608 | tf_op jit(solution)/shard_map/gather_kv/all_to_all | solution.py:179
  44.8 0.0 all-gather.2.cloned.1.call-start
  44.9 0.7 all-gather.2.cloned.1.call-update
  45.6 0.2 reduce-window.9
  45.8 1.4 cache.1
  47.2 0.1 pad_add_fusion.bound_ref
  47.3 45.5 %all-to-all-done = bf16[16,512,256]{2,1,0:T(8,128)(2,1)} async-done(((bf16[16,512,256]{2,1,0:T(8,128)(2,1)}), bf16[16,512,256]{2,1,0:T(8,128)(2,1)}, u32[]{:S(2)}, u32[]{:S(2)}) %all-to-all-start) | async-done | bytes 4194336 | tf_op jit(solution)/shard_map/gather_kv/all_to_all | solution.py:179
  92.8 11.2 %attend.1 = bf16[160,512]{1,0:T(8,128)(2,1)S(1)} custom-call(s32[5]{0:T(128)S(1)} %pad_add_fusion.bound_ref, s32[8]{0:T(128)S(1)} %copy-done.7, s32[1]{0:T(128)} %bitcast.2.first_ref, bf16[128,512]{1,0:T(8,128)(2,1)S(1)} %copy-done.6, bf16[32,512]{1,0:T(8,128)(2,1)S(1)} %bitcast.27, bf16[8192,256]{1,0:T(8,128)(2,1)} %bitcast.4.kv_ref, ...), custom_call_target="tpu_custom_call" | custom-call | flops 2684354560 | bytes 4194304 | tf_op jit(solution)/shard_map/attend/pallas_call | solution.py:214
  104.0 0.9 broadcast_in_dim.5
  104.9 10.4 %all-to-all-start.1 = ((bf16[4,160,512]{2,1,0:T(8,128)(2,1)}), bf16[4,160,512]{2,1,0:T(8,128)(2,1)S(1)}, u32[]{:S(2)}, u32[]{:S(2)}) async-start(bf16[4,160,512]{2,1,0:T(8,128)(2,1)} %broadcast_in_dim.5), calls=%async_computation.1 | async-start | bytes 1310720 | tf_op jit(solution)/shard_map/gather_attn/all_to_all | solution.py:229
  115.3 25.4 %all-gather.2.cloned.1.call-done = bf16[1024,512]{1,0:T(8,128)(2,1)} async-done(((bf16[64,512]{1,0:T(8,128)(2,1)}), bf16[1024,512]{1,0:T(8,128)(2,1)}) %all-gather.2.cloned.1.call-update) | async-done | bytes 1048592 | tf_op jit(solution)/shard_map/gather_weight/all_gather | solution.py:175
  140.7 1.7 convolution_convert_fusion
  142.4 1.9 collective-permute-start
  144.3 2.0 %collective-permute-done = bf16[640,512]{1,0:T(8,128)(2,1)S(1)} collective-permute-done((bf16[640,512]{1,0:T(8,128)(2,1)S(1)}, bf16[640,512]{1,0:T(8,128)(2,1)S(1)}, u32[]{:S(2)}, u32[]{:S(2)}) %collective-permute-start) | collective-permute-done | bytes 655392 | tf_op jit(solution)/shard_map/project/ppermute | solution.py:239
  146.4 0.5 add_convert_fusion
  146.9 0.1 dynamic-slice_bitcast_fusion.3
  147.0 1.9 collective-permute-start.4
  148.9 2.2 %collective-permute-start.3 = (bf16[160,512]{1,0:T(8,128)(2,1)S(1)}, bf16[160,512]{1,0:T(8,128)(2,1)S(1)}, u32[]{:S(2)}, u32[]{:S(2)}) collective-permute-start(bf16[160,512]{1,0:T(8,128)(2,1)S(1)} %get-tuple-element.10), channel_id=1, source_target_pairs={{0,256},{2,384},{4,0},{6,128},{128,258},{130,386},{132,2},{134,130... | collective-permute-start | bytes 491528 | tf_op jit(solution)/shard_map/scatter/ppermute | solution.py:249
  151.1 4.7 %collective-permute-start.2 = (bf16[160,512]{1,0:T(8,128)(2,1)S(1)}, bf16[160,512]{1,0:T(8,128)(2,1)S(1)}, u32[]{:S(2)}, u32[]{:S(2)}) collective-permute-start(bf16[160,512]{1,0:T(8,128)(2,1)S(1)} %get-tuple-element.11), channel_id=1, source_target_pairs={{0,128},{2,256},{4,384},{6,0},{128,130},{130,258},{132,386},{134,2... | collective-permute-start | bytes 491528 | tf_op jit(solution)/shard_map/scatter/ppermute | solution.py:249
  155.9 3.6 %collective-permute-start.1 = (bf16[160,512]{1,0:T(8,128)(2,1)S(1)}, bf16[160,512]{1,0:T(8,128)(2,1)S(1)}, u32[]{:S(2)}, u32[]{:S(2)}) collective-permute-start(bf16[160,512]{1,0:T(8,128)(2,1)S(1)} %get-tuple-element.8), channel_id=1, source_target_pairs={{0,0},{2,128},{4,256},{6,384},{128,2},{130,130},{132,258},{134,386... | collective-permute-start | bytes 491528 | tf_op jit(solution)/shard_map/scatter/ppermute | solution.py:249
  159.5 12.5 %collective-permute-done.4 = bf16[160,512]{1,0:T(8,128)(2,1)S(1)} collective-permute-done((bf16[160,512]{1,0:T(8,128)(2,1)S(1)}, bf16[160,512]{1,0:T(8,128)(2,1)S(1)}, u32[]{:S(2)}, u32[]{:S(2)}) %collective-permute-start.4) | collective-permute-done | bytes 163872 | tf_op jit(solution)/shard_map/scatter/ppermute | solution.py:249
  171.9 21.8 %collective-permute-done.1 = bf16[160,512]{1,0:T(8,128)(2,1)S(1)} collective-permute-done((bf16[160,512]{1,0:T(8,128)(2,1)S(1)}, bf16[160,512]{1,0:T(8,128)(2,1)S(1)}, u32[]{:S(2)}, u32[]{:S(2)}) %collective-permute-start.1) | collective-permute-done | bytes 163872 | tf_op jit(solution)/shard_map/scatter/ppermute | solution.py:249
  193.7 0.1 add_convert_fusion.1
  193.8 0.7 slice.8
  194.5 0.6 slice_bitcast_fusion
  (19 shorter events, 0.0 us)
Async XLA Ops:
  37.2 8.3 %copy-start.9 = (s32[4]{0:T(128)S(1)}, s32[4]{0:T(128)}, u32[]{:S(2)}) copy-start(s32[4]{0:T(128)} %param.15) | copy-start | bytes 52
  37.2 8.5 %copy-start = (bf16[8,256,128]{2,1,0:T(8,128)(2,1)S(1)}, bf16[8,256,128]{2,1,0:T(8,128)(2,1)}, u32[]{:S(2)}) copy-start(bf16[8,256,128]{2,1,0:T(8,128)(2,1)} %param.20) | copy-start | bytes 1572868
  37.3 8.5 %copy-start.1 = (bf16[8,256,128]{2,1,0:T(8,128)(2,1)S(1)}, bf16[8,256,128]{2,1,0:T(8,128)(2,1)}, u32[]{:S(2)}) copy-start(bf16[8,256,128]{2,1,0:T(8,128)(2,1)} %param.21) | copy-start | bytes 1572868
  37.3 8.5 %copy-start.2 = (bf16[4,8,512]{2,1,0:T(8,128)(2,1)S(1)}, bf16[4,8,512]{2,1,0:T(8,128)(2,1)}, u32[]{:S(2)}) copy-start(bf16[4,8,512]{2,1,0:T(8,128)(2,1)} %param.17) | copy-start | bytes 98308
  37.3 8.5 %copy-start.3 = (bf16[4,8,128]{2,1,0:T(8,128)(2,1)S(1)}, bf16[4,8,128]{2,1,0:T(8,128)(2,1)}, u32[]{:S(2)}) copy-start(bf16[4,8,128]{2,1,0:T(8,128)(2,1)} %param.18) | copy-start | bytes 24580
  37.3 8.5 %copy-start.4 = (bf16[4,8,128]{2,1,0:T(8,128)(2,1)S(1)}, bf16[4,8,128]{2,1,0:T(8,128)(2,1)}, u32[]{:S(2)}) copy-start(bf16[4,8,128]{2,1,0:T(8,128)(2,1)} %param.19) | copy-start | bytes 24580
  37.3 8.5 %copy-start.5 = (s32[8]{0:T(128)S(1)}, s32[8]{0:T(128)}, u32[]{:S(2)}) copy-start(s32[8]{0:T(128)} %len_ref.1) | copy-start | bytes 100
  37.3 55.5 %copy-start.6 = (bf16[128,512]{1,0:T(8,128)(2,1)S(1)}, bf16[128,512]{1,0:T(8,128)(2,1)}, u32[]{:S(2)}) copy-start(bf16[128,512]{1,0:T(8,128)(2,1)} %q_ref.1) | copy-start | bytes 393220
  37.3 55.5 %copy-start.7 = (s32[8]{0:T(128)S(1)}, s32[8]{0:T(128)}, u32[]{:S(2)}) copy-start(s32[8]{0:T(128)} %prompt_ref.1) | copy-start | bytes 100
  37.3 55.5 %all-to-all-start = ((bf16[16,512,256]{2,1,0:T(8,128)(2,1)}), bf16[16,512,256]{2,1,0:T(8,128)(2,1)}, u32[]{:S(2)}, u32[]{:S(2)}) async-start(bf16[16,512,256]{2,1,0:T(8,128)(2,1)} %broadcast_in_dim.4), calls=%async_computation | async-start | bytes 8388608 | tf_op jit(solution)/shard_map/gather_kv/all_to_all | solution.py:179
  44.8 95.9 %all-gather.2.cloned.1.call-start = ((), (), s32[]{:S(2)}) async-start(), calls=%async_computation.2 | async-start | bytes 1114112 | tf_op jit(solution)/shard_map/gather_weight/all_gather | solution.py:175
  104.9 35.8 %all-to-all-start.1 = ((bf16[4,160,512]{2,1,0:T(8,128)(2,1)}), bf16[4,160,512]{2,1,0:T(8,128)(2,1)S(1)}, u32[]{:S(2)}, u32[]{:S(2)}) async-start(bf16[4,160,512]{2,1,0:T(8,128)(2,1)} %broadcast_in_dim.5), calls=%async_computation.1 | async-start | bytes 1310720 | tf_op jit(solution)/shard_map/gather_attn/all_to_all | solution.py:229
  140.7 5.7 %copy-start.8 = (bf16[1024,512]{1,0:T(8,128)(2,1)S(1)}, bf16[1024,512]{1,0:T(8,128)(2,1)}, u32[]{:S(2)}) copy-start(bf16[1024,512]{1,0:T(8,128)(2,1)} %all-gather.2.cloned.1.call-done) | copy-start | bytes 3145732
  142.4 4.0 %collective-permute-start = (bf16[640,512]{1,0:T(8,128)(2,1)S(1)}, bf16[640,512]{1,0:T(8,128)(2,1)S(1)}, u32[]{:S(2)}, u32[]{:S(2)}) collective-permute-start(bf16[640,512]{1,0:T(8,128)(2,1)S(1)} %convolution_convert_fusion), channel_id=1, source_target_pairs={{0,1},{1,0},{2,3},{3,2},{4,5},{5,4},{6,7},{7,6},{8,9},{9,8},{10,11... | collective-permute-start | bytes 1966088 | tf_op jit(solution)/shard_map/project/ppermute | solution.py:239
  147.0 24.9 %collective-permute-start.4 = (bf16[160,512]{1,0:T(8,128)(2,1)S(1)}, bf16[160,512]{1,0:T(8,128)(2,1)S(1)}, u32[]{:S(2)}, u32[]{:S(2)}) collective-permute-start(bf16[160,512]{1,0:T(8,128)(2,1)S(1)} %get-tuple-element.9), channel_id=1, source_target_pairs={{0,384},{2,0},{4,128},{6,256},{128,386},{130,2},{132,130},{134,258... | collective-permute-start | bytes 491528 | tf_op jit(solution)/shard_map/scatter/ppermute | solution.py:249
  148.9 23.0 %collective-permute-start.3 = (bf16[160,512]{1,0:T(8,128)(2,1)S(1)}, bf16[160,512]{1,0:T(8,128)(2,1)S(1)}, u32[]{:S(2)}, u32[]{:S(2)}) collective-permute-start(bf16[160,512]{1,0:T(8,128)(2,1)S(1)} %get-tuple-element.10), channel_id=1, source_target_pairs={{0,256},{2,384},{4,0},{6,128},{128,258},{130,386},{132,2},{134,130... | collective-permute-start | bytes 491528 | tf_op jit(solution)/shard_map/scatter/ppermute | solution.py:249
  151.1 20.8 %collective-permute-start.2 = (bf16[160,512]{1,0:T(8,128)(2,1)S(1)}, bf16[160,512]{1,0:T(8,128)(2,1)S(1)}, u32[]{:S(2)}, u32[]{:S(2)}) collective-permute-start(bf16[160,512]{1,0:T(8,128)(2,1)S(1)} %get-tuple-element.11), channel_id=1, source_target_pairs={{0,128},{2,256},{4,384},{6,0},{128,130},{130,258},{132,386},{134,2... | collective-permute-start | bytes 491528 | tf_op jit(solution)/shard_map/scatter/ppermute | solution.py:249
  155.9 37.9 %collective-permute-start.1 = (bf16[160,512]{1,0:T(8,128)(2,1)S(1)}, bf16[160,512]{1,0:T(8,128)(2,1)S(1)}, u32[]{:S(2)}, u32[]{:S(2)}) collective-permute-start(bf16[160,512]{1,0:T(8,128)(2,1)S(1)} %get-tuple-element.8), channel_id=1, source_target_pairs={{0,0},{2,128},{4,256},{6,384},{128,2},{130,130},{132,258},{134,386... | collective-permute-start | bytes 491528 | tf_op jit(solution)/shard_map/scatter/ppermute | solution.py:249
Sparse Core Ops, SparseCore 0:
  48.7 91.9 all-gather.1

commit v2 on v1

v2 whole, which is shorter than its diff:
```python
import math

import jax
import jax.numpy as jnp
from jax import lax
from jax.experimental import pallas as pl
from jax.experimental.pallas import tpu as pltpu
from jax.sharding import Mesh, PartitionSpec as P

HD = 128
GROUP = 4
STEPS = 4
SIDE = 4
BLOCK = 2048
MASKED = -1e30
SCALE = math.log2(math.e) / math.sqrt(HD)


def fold(state, queries, keys, values, visible):
    top, total, acc = state
    scores = lax.dot_general(
        queries, keys, (((1,), (1,)), ((), ())), preferred_element_type=jnp.float32
    )
    scores = scores * SCALE
    if visible is not None:
        scores = jnp.where(visible, scores, MASKED)
    new_top = jnp.maximum(top, jnp.max(scores, axis=1, keepdims=True))
    weights = jnp.exp2(scores - new_top)
    factor = jnp.exp2(top - new_top)
    total = total * factor + jnp.sum(weights, axis=1, keepdims=True)
    acc = acc * factor + jnp.dot(
        weights.astype(jnp.bfloat16), values, preferred_element_type=jnp.float32
    )
    return new_top, total, acc


def by_head(ref):
    return jnp.concatenate([ref[:, h * HD : (h + 1) * HD] for h in range(GROUP)], axis=0)


def cache_kernel(len_ref, q_ref, nk_ref, nv_ref, ck_ref, cv_ref, top_ref, total_ref, acc_ref):
    rows = len_ref.shape[0]
    keys = ck_ref.shape[0]
    slots = keys // rows
    new = nk_ref.shape[0]
    queries = by_head(q_ref)
    count = queries.shape[0]
    index = lax.broadcasted_iota(jnp.int32, (count, 1), 0)
    row = lax.rem(index, rows)
    step = lax.rem(index // rows, STEPS)
    state = (
        jnp.full((count, 1), MASKED, jnp.float32),
        jnp.zeros((count, 1), jnp.float32),
        jnp.zeros((count, HD), jnp.float32),
    )
    key = lax.broadcasted_iota(jnp.int32, (count, new), 1)
    seen = (lax.rem(key, rows) == row) & (key // rows <= step)
    state = fold(state, queries, nk_ref[...], nv_ref[...], seen)
    low = row * slots
    high = low
    for r in range(rows):
        high = jnp.where(row == r, low + len_ref[r], high)
    key = lax.broadcasted_iota(jnp.int32, (count, keys), 1)
    state = fold(state, queries, ck_ref[...], cv_ref[...], (key >= low) & (key < high))
    top_ref[...] = state[0]
    total_ref[...] = state[1]
    acc_ref[...] = state[2]


def prompt_kernel(
    bound_ref,
    prompt_ref,
    first_ref,
    q_ref,
    dq_ref,
    kv_ref,
    top_ref,
    total_ref,
    acc_ref,
    out_ref,
    queries,
    low,
    high,
    top,
    total,
    acc,
):
    prompts = bound_ref.shape[0] - 1
    rows = prompt_ref.shape[0]
    tokens = q_ref.shape[0]
    split = tokens * GROUP
    count = queries.shape[0]
    step = pl.program_id(0)
    first = first_ref[0]
    last = first + tokens - 1
    first_low = jnp.int32(0)
    last_low = jnp.int32(0)
    for b in range(1, prompts):
        first_low = jnp.where(first >= bound_ref[b], bound_ref[b], first_low)
        last_low = jnp.where(last >= bound_ref[b], bound_ref[b], last_low)

    @pl.when(step == 0)
    def _():
        queries[:split] = by_head(q_ref)
        queries[split:] = by_head(dq_ref)
        top[:split] = jnp.full((split, 1), MASKED, jnp.float32)
        total[:split] = jnp.zeros((split, 1), jnp.float32)
        acc[:split] = jnp.zeros((split, HD), jnp.float32)
        top[split:] = top_ref[...]
        total[split:] = total_ref[...]
        acc[split:] = acc_ref[...]
        pos = first + lax.rem(lax.broadcasted_iota(jnp.int32, (split, 1), 0), tokens)
        begin = jnp.zeros((split, 1), jnp.int32)
        for b in range(1, prompts):
            begin = jnp.where(pos >= bound_ref[b], bound_ref[b], begin)
        low[:split] = begin
        high[:split] = pos + 1
        row = lax.rem(lax.broadcasted_iota(jnp.int32, (count - split, 1), 0), rows)
        begin = jnp.zeros((count - split, 1), jnp.int32)
        end = begin
        for r in range(rows):
            which = prompt_ref[r]
            begin = jnp.where(row == r, bound_ref[which], begin)
            end = jnp.where(row == r, bound_ref[which + 1], end)
        low[split:] = begin
        high[split:] = end

    start = step * BLOCK

    def visit(part, masked):
        visible = None
        if masked:
            pos = start + lax.broadcasted_iota(jnp.int32, (part.stop - part.start, BLOCK), 1)
            visible = (pos >= low[part]) & (pos < high[part])
        top[part], total[part], acc[part] = fold(
            (top[part], total[part], acc[part]),
            queries[part],
            kv_ref[:, :HD],
            kv_ref[:, HD:],
            visible,
        )

    prefill, decode = slice(0, split), slice(split, count)
    near = (start + BLOCK > first_low) & (start <= last)
    full = (start >= last_low) & (start + BLOCK <= first + 1)

    @pl.when(jnp.logical_not(near))
    def _():
        visit(decode, True)

    @pl.when(near & full)
    def _():
        visit(decode, True)
        visit(prefill, False)

    @pl.when(near & jnp.logical_not(full))
    def _():
        visit(decode, True)
        visit(prefill, True)

    @pl.when(step == pl.num_programs(0) - 1)
    def _():
        done = (acc[...] / total[...]).astype(jnp.bfloat16)
        each = (count - split) // GROUP
        for h in range(GROUP):
            columns = slice(h * HD, (h + 1) * HD)
            out_ref[:tokens, columns] = done[h * tokens : (h + 1) * tokens]
            out_ref[tokens:, columns] = done[split + h * each : split + (h + 1) * each]


def body(
    pre_query,
    pre_key,
    pre_value,
    prompt_lengths,
    out_weight,
    dec_query,
    dec_key,
    dec_value,
    cache_key,
    cache_value,
    cache_lengths,
    row_prompt,
):
    tokens = pre_query.shape[0]
    steps, rows, width = dec_query.shape
    slots = cache_key.shape[1]
    H, L = lax.axis_size("zh"), lax.axis_size("zl")
    x, y, zh, core = (lax.axis_index(a) for a in ("x", "y", "zh", "core"))
    smem = pl.BlockSpec(memory_space=pltpu.SMEM)
    vmem = pl.BlockSpec(memory_space=pltpu.VMEM)
    params = pltpu.CompilerParams(vmem_limit_bytes=40 * 2**20)

    def spread(v, axis, count=SIDE):
        return lax.all_to_all(jnp.broadcast_to(v[None], (count,) + v.shape), axis, 0, 0)

    def collect(v, axis):
        near = [v]
        for k in range(1, SIDE):
            near.append(lax.ppermute(v, axis, [(i, (i - k) % SIDE) for i in range(SIDE)]))
        twice = jnp.stack(near + near)
        return lax.dynamic_slice_in_dim(twice, SIDE - lax.axis_index(axis), SIDE, 0)

    with jax.named_scope("gather_kv"):
        kv = jnp.concatenate([pre_key, pre_value], axis=1)
        kv = lax.all_gather(kv, "zh", axis=0, tiled=True)
    with jax.named_scope("gather_weight_near"):
        weight, kv = lax.optimization_barrier((out_weight.T, kv))
        weight = collect(weight, "zh")
    with jax.named_scope("gather_kv"):
        kv = spread(kv, ("x", "y"), SIDE * SIDE).reshape(-1, 2 * HD)
    with jax.named_scope("gather_weight"):
        weight, kv = lax.optimization_barrier((weight, kv))
        weight = spread(weight, "x")
        weight = weight.reshape(SIDE, 2, -1, weight.shape[-1])

    dq = dec_query.reshape(steps * rows, width)
    lanes = steps * rows * GROUP
    with jax.named_scope("cache"):
        state = pl.pallas_call(
            cache_kernel,
            out_shape=(
                jax.ShapeDtypeStruct((lanes, 1), jnp.float32),
                jax.ShapeDtypeStruct((lanes, 1), jnp.float32),
                jax.ShapeDtypeStruct((lanes, HD), jnp.float32),
            ),
            in_specs=[smem] + [vmem] * 5,
            out_specs=(vmem, vmem, vmem),
            compiler_params=params,
            cost_estimate=pl.CostEstimate(
                flops=4 * lanes * HD * rows * slots,
                bytes_accessed=4 * rows * slots * HD,
                transcendentals=lanes * rows * slots,
            ),
        )(
            cache_lengths,
            dq,
            dec_key.reshape(steps * rows, HD),
            dec_value.reshape(steps * rows, HD),
            cache_key.reshape(rows * slots, HD),
            cache_value.reshape(rows * slots, HD),
        )

    bounds = jnp.concatenate([jnp.zeros((1,), jnp.int32), jnp.cumsum(prompt_lengths)]).astype(
        jnp.int32
    )
    first = (((x * SIDE + y) * H + zh) * tokens).astype(jnp.int32).reshape(1)
    count = tokens * GROUP + lanes

    def whole(*shape):
        return pl.BlockSpec(shape, lambda i: (0,) * len(shape))

    with jax.named_scope("attend"):
        attn = pl.pallas_call(
            prompt_kernel,
            out_shape=jax.ShapeDtypeStruct((tokens + steps * rows, width), jnp.bfloat16),
            grid=(kv.shape[0] // BLOCK,),
            in_specs=[smem] * 3
            + [
                whole(tokens, width),
                whole(steps * rows, width),
                pl.BlockSpec((BLOCK, 2 * HD), lambda i: (i, 0)),
                whole(lanes, 1),
                whole(lanes, 1),
                whole(lanes, HD),
            ],
            out_specs=whole(tokens + steps * rows, width),
            scratch_shapes=[
                pltpu.VMEM((count, HD), jnp.bfloat16),
                pltpu.VMEM((count, 1), jnp.int32),
                pltpu.VMEM((count, 1), jnp.int32),
                pltpu.VMEM((count, 1), jnp.float32),
                pltpu.VMEM((count, 1), jnp.float32),
                pltpu.VMEM((count, HD), jnp.float32),
            ],
            compiler_params=params,
            cost_estimate=pl.CostEstimate(
                flops=4 * count * HD * kv.shape[0],
                bytes_accessed=2 * kv.size,
                transcendentals=count * kv.shape[0],
            ),
        )(bounds, row_prompt, first, pre_query, dq, kv, *state)

    total = attn.shape[0]
    with jax.named_scope("gather_attn"):
        attn = spread(attn, "y").reshape(SIDE * total, width)
    with jax.named_scope("project"):
        def product(which):
            part = lax.dynamic_index_in_dim(weight, which, 1, keepdims=False)
            return lax.dot_general(
                attn,
                part.reshape(-1, width),
                (((1,), (1,)), ((), ())),
                preferred_element_type=jnp.float32,
            ).astype(jnp.bfloat16)

        swap = [(0, 1), (1, 0)]
        other = lax.ppermute(product(1 - core), "core", swap)
        mine = product(core)
        mine = (mine.astype(jnp.float32) + other.astype(jnp.float32)).astype(jnp.bfloat16)
    with jax.named_scope("scatter"):
        pieces = mine.reshape(SIDE, total, L, HD).transpose(0, 2, 1, 3)
        pieces = lax.all_to_all(pieces.reshape(SIDE * L, total, HD), ("y", "zl"), 0, 0)
        pieces = pieces.reshape(2, 2, L, total, HD)
        pieces = jnp.sum(pieces.astype(jnp.float32), axis=2).astype(jnp.bfloat16)
        keep = lax.dynamic_index_in_dim(pieces, core, 0, keepdims=False)
        give = lax.dynamic_index_in_dim(pieces, 1 - core, 0, keepdims=False)
        take = lax.ppermute(give, "core", swap)
        low = jnp.where(core == 0, keep, take)
        high = jnp.where(core == 0, take, keep)
        result = jnp.concatenate([low[0], high[0], low[1], high[1]], axis=-1)
    return result[:tokens], result[tokens:].reshape(steps, rows, result.shape[1])


def solution(mesh):
    fine = Mesh(mesh.devices.reshape(4, 4, 4, 4, 2), ("x", "y", "zh", "zl", "core"))
    seq, tensor = ("x", "y", "zh"), ("zl", "core")
    placed = (
        P(seq, tensor),
        P(seq, tensor),
        P(seq, tensor),
        P(),
        P(tensor, seq),
        P(None, seq, tensor),
        P(None, seq, tensor),
        P(None, seq, tensor),
        P(seq, None, tensor),
        P(seq, None, tensor),
        P(seq),
        P(seq),
    )
    return jax.shard_map(
        body,
        mesh=fine,
        in_specs=placed,
        out_specs=(P(seq, tensor), P(None, seq, tensor)),
        check_vma=False,
    )
```

time: 202 us -> 156 us (0.77)
  the two profiles are of different devices: /device:TPU:10 before, /device:TPU:1 now
where the time goes in v2:
time: 156 us; the launch traced here: 154 us
  blocking collectives  47.6 us (31%)
  starting transfers between devices  47 us (30%)
  waiting for transfers between devices  40.7 us (26%)
  Pallas kernels  9.28 us (6%)
  local copies, waits for them, and re-layouts  5.53 us (4%)
  other arithmetic  1.78 us (1%)
    all_to_all x3, waiting for transfers between devices, spread(): lax.all_to_all(jnp.broadcast_to(v[None], (count,) + v.shape), axis, 0, 0)  30.7 us
    all_gather x1, blocking collectives, body(): kv = lax.all_gather(kv, 'zh', axis=0, tiled=True)  25.3 us
    all_to_all x1, blocking collectives, body(): lax.all_to_all(pieces.reshape(SIDE * L, total, HD), ('y', 'zl'), 0, 0)  22.3 us
    all_to_all x3, starting transfers between devices, spread(): lax.all_to_all(jnp.broadcast_to(v[None], (count,) + v.shape), axis, 0, 0)  18.3 us
    ppermute x3, starting transfers between devices, collect(): lax.ppermute(v, axis, [(i, (i - k) % SIDE) for i in range(SIDE)])  16.2 us
    ppermute x1, starting transfers between devices, body(): other = lax.ppermute(product(1 - core), 'core', swap)  9.13 us
    pallas_call x1, Pallas kernels, body(): pl.pallas_call(prompt_kernel, out_shape=jax.ShapeDtypeStruct((tokens + st...  7.73 us
    ppermute x3, waiting for transfers between devices, collect(): lax.ppermute(v, axis, [(i, (i - k) % SIDE) for i in range(SIDE)])  7.44 us
  transfers between devices with their start and end apart: 8, of which 7 were waited for; matrix products, arithmetic and copies ran while one was open for 0% of the time, Pallas kernels for 6%

profile of v2, /device:TPU:1, one launch (start us, length us, event | category | flops | bytes accessed | tf_op | source)
XLA Modules:
  0.0 153.9 jit_solution(17910432364334884283)
XLA Ops:
  0.6 0.8 pad_maximum_fusion.1
  1.4 25.3 %all_gather.3 = bf16[512,256]{1,0:T(8,128)(2,1)S(1)} all-gather(bf16[128,256]{1,0:T(8,128)(2,1)S(1)} %pad_maximum_fusion.1), channel_id=1, replica_groups=mesh['x'=4,'y'=4,'zh'=4,'zl'=4,'core'=2] {'zh'}, dimensions={0}, use_global_device_ids=true | all-gather | bytes 327680 | tf_op jit(solution)/shard_map/gather_kv/all_gather | solution.py:206
  26.7 2.4 %broadcast_in_dim.6 = bf16[16,512,256]{2,1,0:T(8,128)(2,1)} broadcast(bf16[512,256]{1,0:T(8,128)(2,1)S(1)} %all_gather.3), dimensions={1,2} | broadcast | bytes 4456448 | tf_op jit(solution)/shard_map/gather_kv/broadcast_in_dim | solution.py:195
  29.1 6.9 %all-to-all-start = ((bf16[16,512,256]{2,1,0:T(8,128)(2,1)}), bf16[16,512,256]{2,1,0:T(8,128)(2,1)}, u32[]{:S(2)}, u32[]{:S(2)}) async-start(bf16[16,512,256]{2,1,0:T(8,128)(2,1)} %broadcast_in_dim.6), calls=%async_computation | async-start | bytes 8388608 | tf_op jit(solution)/shard_map/gather_kv/all_to_all | solution.py:195
  36.0 4.7 %collective-permute-start = (bf16[64,512]{1,0:T(8,128)(2,1)S(1)}, bf16[64,512]{1,0:T(8,128)(2,1)S(1)}, u32[]{:S(2)}, u32[]{:S(2)}) collective-permute-start(bf16[64,512]{1,0:T(8,128)(2,1)S(1)} %bitcast.62), channel_id=1, source_target_pairs={{0,24},{8,0},{16,8},{24,16},{1,25},{9,1},{17,9},{25,17},{2,26},{10... | collective-permute-start | bytes 196616 | tf_op jit(solution)/shard_map/gather_weight_near/ppermute | solution.py:200
  40.8 6.9 %collective-permute-start.1 = (bf16[64,512]{1,0:T(8,128)(2,1)S(1)}, bf16[64,512]{1,0:T(8,128)(2,1)S(1)}, u32[]{:S(2)}, u32[]{:S(2)}) collective-permute-start(bf16[64,512]{1,0:T(8,128)(2,1)S(1)} %bitcast.63), channel_id=1, source_target_pairs={{0,16},{8,24},{16,0},{24,8},{1,17},{9,25},{17,1},{25,9},{2,18},{10... | collective-permute-start | bytes 196616 | tf_op jit(solution)/shard_map/gather_weight_near/ppermute | solution.py:200
  47.7 4.5 %collective-permute-start.2 = (bf16[64,512]{1,0:T(8,128)(2,1)S(1)}, bf16[64,512]{1,0:T(8,128)(2,1)S(1)}, u32[]{:S(2)}, u32[]{:S(2)}) collective-permute-start(bf16[64,512]{1,0:T(8,128)(2,1)S(1)} %bitcast.64), channel_id=1, source_target_pairs={{0,8},{8,16},{16,24},{24,0},{1,9},{9,17},{17,25},{25,1},{2,10},{10... | collective-permute-start | bytes 196616 | tf_op jit(solution)/shard_map/gather_weight_near/ppermute | solution.py:200
  52.3 2.3 %collective-permute-done.1 = bf16[64,512]{1,0:T(8,128)(2,1)S(1)} collective-permute-done((bf16[64,512]{1,0:T(8,128)(2,1)S(1)}, bf16[64,512]{1,0:T(8,128)(2,1)S(1)}, u32[]{:S(2)}, u32[]{:S(2)}) %collective-permute-start.1) | collective-permute-done | bytes 65568 | tf_op jit(solution)/shard_map/gather_weight_near/ppermute | solution.py:200
  54.6 5.2 %collective-permute-done.2 = bf16[64,512]{1,0:T(8,128)(2,1)S(1)} collective-permute-done((bf16[64,512]{1,0:T(8,128)(2,1)S(1)}, bf16[64,512]{1,0:T(8,128)(2,1)S(1)}, u32[]{:S(2)}, u32[]{:S(2)}) %collective-permute-start.2) | collective-permute-done | bytes 65568 | tf_op jit(solution)/shard_map/gather_weight_near/ppermute | solution.py:200
  59.8 23.0 %all-to-all-done = bf16[16,512,256]{2,1,0:T(8,128)(2,1)} async-done(((bf16[16,512,256]{2,1,0:T(8,128)(2,1)}), bf16[16,512,256]{2,1,0:T(8,128)(2,1)}, u32[]{:S(2)}, u32[]{:S(2)}) %all-to-all-start) | async-done | bytes 4194336 | tf_op jit(solution)/shard_map/gather_kv/all_to_all | solution.py:195
  82.8 1.1 broadcast_in_dim.8
  83.9 6.9 %all-to-all-start.2 = ((bf16[4,4,64,512]{3,2,1,0:T(8,128)(2,1)}), bf16[4,4,64,512]{3,2,1,0:T(8,128)(2,1)S(1)}, u32[]{:S(2)}, u32[]{:S(2)}) async-start(bf16[4,4,64,512]{3,2,1,0:T(8,128)(2,1)} %broadcast_in_dim.8), calls=%async_computation.2 | async-start | bytes 2097152 | tf_op jit(solution)/shard_map/gather_weight/all_to_all | solution.py:195
  90.8 0.2 reduce-window.9
  91.0 1.5 %cache.1 = (f32[128,1]{1,0:T(8,128)S(1)}, f32[128,1]{1,0:T(8,128)S(1)}, f32[128,128]{1,0:T(8,128)S(1)}) custom-call(s32[8]{0:T(128)S(1)} %copy-done.5, bf16[32,512]{1,0:T(8,128)(2,1)S(1)} %bitcast.52, bf16[32,128]{1,0:T(8,128)(2,1)S(1)} %bitcast.54, bf16[32,128]{1,0:T(8,128)(2,1)S(1)} %bitcast.55, bf16[2048,128]{1,0:T(8,128)(2,1)S(1)} %bitcast.50, ...), custom_call_target="tpu_custom_call" | custom-call | flops 134217728 | bytes 1048576 | tf_op jit(solution)/shard_map/cache/pallas_call | solution.py:220
  92.6 7.7 %attend.1 = bf16[160,512]{1,0:T(8,128)(2,1)S(1)} custom-call(s32[5]{0:T(128)S(1)} %pad_add_fusion.bound_ref, s32[8]{0:T(128)S(1)} %copy-done.7, s32[1]{0:T(128)} %bitcast.2.first_ref, bf16[128,512]{1,0:T(8,128)(2,1)S(1)} %copy-done.6, bf16[32,512]{1,0:T(8,128)(2,1)S(1)} %bitcast.53, bf16[8192,256]{1,0:T(8,128)(2,1)} %bitcast.9.kv_ref, ...), custom_call_target="tpu_custom_call" | custom-call | flops 2684354560 | bytes 4194304 | tf_op jit(solution)/shard_map/attend/pallas_call | solution.py:254
  100.4 0.2 all-to-all-done.2
  100.5 0.9 broadcast_in_dim.7
  101.4 4.5 %all-to-all-start.1 = ((bf16[4,160,512]{2,1,0:T(8,128)(2,1)}), bf16[4,160,512]{2,1,0:T(8,128)(2,1)S(1)}, u32[]{:S(2)}, u32[]{:S(2)}) async-start(bf16[4,160,512]{2,1,0:T(8,128)(2,1)} %broadcast_in_dim.7), calls=%async_computation.1 | async-start | bytes 1310720 | tf_op jit(solution)/shard_map/gather_attn/all_to_all | solution.py:195
  106.0 0.1 constant_dynamic-slice_fusion
  106.1 7.5 %all-to-all-done.1 = bf16[4,160,512]{2,1,0:T(8,128)(2,1)S(1)} async-done(((bf16[4,160,512]{2,1,0:T(8,128)(2,1)}), bf16[4,160,512]{2,1,0:T(8,128)(2,1)S(1)}, u32[]{:S(2)}, u32[]{:S(2)}) %all-to-all-start.1) | async-done | bytes 655392 | tf_op jit(solution)/shard_map/gather_attn/all_to_all | solution.py:195
  113.6 0.5 convolution_convert_fusion
  114.2 9.1 %collective-permute-start.3 = (bf16[640,512]{1,0:T(8,128)(2,1)S(1)}, bf16[640,512]{1,0:T(8,128)(2,1)S(1)}, u32[]{:S(2)}, u32[]{:S(2)}) collective-permute-start(bf16[640,512]{1,0:T(8,128)(2,1)S(1)} %convolution_convert_fusion), channel_id=1, source_target_pairs={{0,1},{1,0},{2,3},{3,2},{4,5},{5,4},{6,7},{7,6},{8,9},{9,8},{10,11... | collective-permute-start | bytes 1966088 | tf_op jit(solution)/shard_map/project/ppermute | solution.py:298
  123.3 1.7 %collective-permute-done.3 = bf16[640,512]{1,0:T(8,128)(2,1)S(1)} collective-permute-done((bf16[640,512]{1,0:T(8,128)(2,1)S(1)}, bf16[640,512]{1,0:T(8,128)(2,1)S(1)}, u32[]{:S(2)}, u32[]{:S(2)}) %collective-permute-start.3) | collective-permute-done | bytes 655392 | tf_op jit(solution)/shard_map/project/ppermute | solution.py:298
  125.0 0.5 add_convert_fusion
  125.5 0.2 reshape.93
  125.7 0.1 copy.14
  125.8 22.3 %all_to_all.20 = bf16[16,160,128]{2,1,0:T(8,128)(2,1)S(1)} all-to-all(bf16[16,160,128]{2,1,0:T(8,128)(2,1)S(1)} %bitcast.57), channel_id=1, replica_groups=mesh['x'=4,'y'=4,'zh'=4,'zl'=4,'core'=2] {'y','zl'}, dimensions={0} | all-to-all | bytes 1310720 | tf_op jit(solution)/shard_map/scatter/all_to_all | solution.py:303
  148.2 0.1 bitcast_reduce_fusion
  148.3 3.3 %collective-permute-start.4 = (bf16[2,160,128]{2,1,0:T(8,128)(2,1)S(1)}, bf16[2,160,128]{2,1,0:T(8,128)(2,1)S(1)}, u32[]{:S(2)}, u32[]{:S(2)}) collective-permute-start(bf16[2,160,128]{2,1,0:T(8,128)(2,1)S(1)} %dynamic-slice_bitcast_fusion), channel_id=1, source_target_pairs={{0,1},{1,0},{2,3},{3,2},{4,5},{5,4},{6,7},{7,6},{8,9},{9,8},{10,11... | collective-permute-start | bytes 245768 | tf_op jit(solution)/shard_map/scatter/ppermute | solution.py:308
  151.6 0.9 collective-permute-done.4
  152.5 0.6 maximum_bitcast_fusion
  153.2 0.7 slice.28
  (35 shorter events, 0.3 us)
Async XLA Ops:
  29.1 6.9 %copy-start.8 = (bf16[512,64]{0,1:T(8,128)(2,1)S(1)}, bf16[512,64]{0,1:T(8,128)(2,1)}, u32[]{:S(2)}) copy-start(bf16[512,64]{0,1:T(8,128)(2,1)} %param.16) | copy-start | bytes 196612
  29.1 53.7 %all-to-all-start = ((bf16[16,512,256]{2,1,0:T(8,128)(2,1)}), bf16[16,512,256]{2,1,0:T(8,128)(2,1)}, u32[]{:S(2)}, u32[]{:S(2)}) async-start(bf16[16,512,256]{2,1,0:T(8,128)(2,1)} %broadcast_in_dim.6), calls=%async_computation | async-start | bytes 8388608 | tf_op jit(solution)/shard_map/gather_kv/all_to_all | solution.py:195
  36.0 16.2 %collective-permute-start = (bf16[64,512]{1,0:T(8,128)(2,1)S(1)}, bf16[64,512]{1,0:T(8,128)(2,1)S(1)}, u32[]{:S(2)}, u32[]{:S(2)}) collective-permute-start(bf16[64,512]{1,0:T(8,128)(2,1)S(1)} %bitcast.62), channel_id=1, source_target_pairs={{0,24},{8,0},{16,8},{24,16},{1,25},{9,1},{17,9},{25,17},{2,26},{10... | collective-permute-start | bytes 196616 | tf_op jit(solution)/shard_map/gather_weight_near/ppermute | solution.py:200
  40.8 13.8 %collective-permute-start.1 = (bf16[64,512]{1,0:T(8,128)(2,1)S(1)}, bf16[64,512]{1,0:T(8,128)(2,1)S(1)}, u32[]{:S(2)}, u32[]{:S(2)}) collective-permute-start(bf16[64,512]{1,0:T(8,128)(2,1)S(1)} %bitcast.63), channel_id=1, source_target_pairs={{0,16},{8,24},{16,0},{24,8},{1,17},{9,25},{17,1},{25,9},{2,18},{10... | collective-permute-start | bytes 196616 | tf_op jit(solution)/shard_map/gather_weight_near/ppermute | solution.py:200
  47.7 12.0 %collective-permute-start.2 = (bf16[64,512]{1,0:T(8,128)(2,1)S(1)}, bf16[64,512]{1,0:T(8,128)(2,1)S(1)}, u32[]{:S(2)}, u32[]{:S(2)}) collective-permute-start(bf16[64,512]{1,0:T(8,128)(2,1)S(1)} %bitcast.64), channel_id=1, source_target_pairs={{0,8},{8,16},{16,24},{24,0},{1,9},{9,17},{17,25},{25,1},{2,10},{10... | collective-permute-start | bytes 196616 | tf_op jit(solution)/shard_map/gather_weight_near/ppermute | solution.py:200
  83.9 6.9 %copy-start.9 = (s32[4]{0:T(128)S(1)}, s32[4]{0:T(128)}, u32[]{:S(2)}) copy-start(s32[4]{0:T(128)} %param.15) | copy-start | bytes 52
  83.9 7.1 %copy-start = (bf16[8,256,128]{2,1,0:T(8,128)(2,1)S(1)}, bf16[8,256,128]{2,1,0:T(8,128)(2,1)}, u32[]{:S(2)}) copy-start(bf16[8,256,128]{2,1,0:T(8,128)(2,1)} %param.20) | copy-start | bytes 1572868
  83.9 7.1 %copy-start.1 = (bf16[8,256,128]{2,1,0:T(8,128)(2,1)S(1)}, bf16[8,256,128]{2,1,0:T(8,128)(2,1)}, u32[]{:S(2)}) copy-start(bf16[8,256,128]{2,1,0:T(8,128)(2,1)} %param.21) | copy-start | bytes 1572868
  83.9 7.1 %copy-start.2 = (bf16[4,8,512]{2,1,0:T(8,128)(2,1)S(1)}, bf16[4,8,512]{2,1,0:T(8,128)(2,1)}, u32[]{:S(2)}) copy-start(bf16[4,8,512]{2,1,0:T(8,128)(2,1)} %param.17) | copy-start | bytes 98308
  83.9 7.1 %copy-start.3 = (bf16[4,8,128]{2,1,0:T(8,128)(2,1)S(1)}, bf16[4,8,128]{2,1,0:T(8,128)(2,1)}, u32[]{:S(2)}) copy-start(bf16[4,8,128]{2,1,0:T(8,128)(2,1)} %param.18) | copy-start | bytes 24580
  83.9 7.1 %copy-start.4 = (bf16[4,8,128]{2,1,0:T(8,128)(2,1)S(1)}, bf16[4,8,128]{2,1,0:T(8,128)(2,1)}, u32[]{:S(2)}) copy-start(bf16[4,8,128]{2,1,0:T(8,128)(2,1)} %param.19) | copy-start | bytes 24580
  83.9 7.1 %copy-start.5 = (s32[8]{0:T(128)S(1)}, s32[8]{0:T(128)}, u32[]{:S(2)}) copy-start(s32[8]{0:T(128)} %len_ref.1) | copy-start | bytes 100
  83.9 8.7 %copy-start.6 = (bf16[128,512]{1,0:T(8,128)(2,1)S(1)}, bf16[128,512]{1,0:T(8,128)(2,1)}, u32[]{:S(2)}) copy-start(bf16[128,512]{1,0:T(8,128)(2,1)} %q_ref.1) | copy-start | bytes 393220
  83.9 8.7 %copy-start.7 = (s32[8]{0:T(128)S(1)}, s32[8]{0:T(128)}, u32[]{:S(2)}) copy-start(s32[8]{0:T(128)} %prompt_ref.1) | copy-start | bytes 100
  83.9 16.6 %all-to-all-start.2 = ((bf16[4,4,64,512]{3,2,1,0:T(8,128)(2,1)}), bf16[4,4,64,512]{3,2,1,0:T(8,128)(2,1)S(1)}, u32[]{:S(2)}, u32[]{:S(2)}) async-start(bf16[4,4,64,512]{3,2,1,0:T(8,128)(2,1)} %broadcast_in_dim.8), calls=%async_computation.2 | async-start | bytes 2097152 | tf_op jit(solution)/shard_map/gather_weight/all_to_all | solution.py:195
  101.4 12.2 %all-to-all-start.1 = ((bf16[4,160,512]{2,1,0:T(8,128)(2,1)}), bf16[4,160,512]{2,1,0:T(8,128)(2,1)S(1)}, u32[]{:S(2)}, u32[]{:S(2)}) async-start(bf16[4,160,512]{2,1,0:T(8,128)(2,1)} %broadcast_in_dim.7), calls=%async_computation.1 | async-start | bytes 1310720 | tf_op jit(solution)/shard_map/gather_attn/all_to_all | solution.py:195
  114.2 10.8 %collective-permute-start.3 = (bf16[640,512]{1,0:T(8,128)(2,1)S(1)}, bf16[640,512]{1,0:T(8,128)(2,1)S(1)}, u32[]{:S(2)}, u32[]{:S(2)}) collective-permute-start(bf16[640,512]{1,0:T(8,128)(2,1)S(1)} %convolution_convert_fusion), channel_id=1, source_target_pairs={{0,1},{1,0},{2,3},{3,2},{4,5},{5,4},{6,7},{7,6},{8,9},{9,8},{10,11... | collective-permute-start | bytes 1966088 | tf_op jit(solution)/shard_map/project/ppermute | solution.py:298
  148.3 4.2 %collective-permute-start.4 = (bf16[2,160,128]{2,1,0:T(8,128)(2,1)S(1)}, bf16[2,160,128]{2,1,0:T(8,128)(2,1)S(1)}, u32[]{:S(2)}, u32[]{:S(2)}) collective-permute-start(bf16[2,160,128]{2,1,0:T(8,128)(2,1)S(1)} %dynamic-slice_bitcast_fusion), channel_id=1, source_target_pairs={{0,1},{1,0},{2,3},{3,2},{4,5},{5,4},{6,7},{7,6},{8,9},{9,8},{10,11... | collective-permute-start | bytes 245768 | tf_op jit(solution)/shard_map/scatter/ppermute | solution.py:308

commit v3 on v2

v3 whole, which is shorter than its diff:
```python
import functools
import math

import jax
import jax.numpy as jnp
from jax import lax
from jax.experimental import pallas as pl
from jax.experimental.pallas import tpu as pltpu
from jax.sharding import Mesh, PartitionSpec as P

HD = 128
GROUP = 4
STEPS = 4
SIDE = 4
TOKENS = 128
MASKED = -1e30
SCALE = math.log2(math.e) / math.sqrt(HD)


def fold(queries, keys, values, visible):
    scores = lax.dot_general(
        queries, keys, (((1,), (1,)), ((), ())), preferred_element_type=jnp.float32
    )
    scores = scores * SCALE
    if visible is not None:
        scores = jnp.where(visible, scores, MASKED)
    top = jnp.max(scores, axis=1, keepdims=True)
    weights = jnp.exp2(scores - top)
    total = jnp.sum(weights, axis=1, keepdims=True)
    acc = jnp.dot(weights.astype(jnp.bfloat16), values, preferred_element_type=jnp.float32)
    return acc / total, top + jnp.log2(total)


def by_head(block):
    return jnp.concatenate([block[:, h * HD : (h + 1) * HD] for h in range(GROUP)], axis=0)


def cache_kernel(len_ref, q_ref, nk_ref, nv_ref, ck_ref, cv_ref, out_ref, log_ref):
    rows = len_ref.shape[0]
    keys = ck_ref.shape[0]
    slots = keys // rows
    new = nk_ref.shape[0]
    queries = by_head(q_ref[...])
    count = queries.shape[0]
    index = lax.broadcasted_iota(jnp.int32, (count, 1), 0)
    row = lax.rem(index, rows)
    step = lax.rem(index // rows, STEPS)
    key = lax.broadcasted_iota(jnp.int32, (count, new), 1)
    seen = (lax.rem(key, rows) == row) & (key // rows <= step)
    new_out, new_log = fold(queries, nk_ref[...], nv_ref[...], seen)
    low = row * slots
    high = low
    for r in range(rows):
        high = jnp.where(row == r, low + len_ref[r], high)
    key = lax.broadcasted_iota(jnp.int32, (count, keys), 1)
    old_out, old_log = fold(queries, ck_ref[...], cv_ref[...], (key >= low) & (key < high))
    top = jnp.maximum(new_log, old_log)
    new_share, old_share = jnp.exp2(new_log - top), jnp.exp2(old_log - top)
    total = new_share + old_share
    out_ref[...] = (new_out * new_share + old_out * old_share) / total
    log_ref[...] = top + jnp.log2(total)


def stamp(logs):
    lane = lax.broadcasted_iota(jnp.int32, (logs[0].shape[0], HD), 1)
    tile = jnp.zeros(lane.shape, jnp.float32)
    for h, column in enumerate(logs):
        for part in range(3):
            piece = column.astype(jnp.bfloat16).astype(jnp.float32)
            tile = jnp.where(lane == 3 * h + part, piece, tile)
            column = column - piece
    return tile.astype(jnp.bfloat16)


def prompt_kernel(bound_ref, place_ref, q0_ref, q1_ref, q2_ref, q3_ref, kv_ref, out_ref, asked_ref):
    prompts = bound_ref.shape[0] - 1
    keys = kv_ref.shape[0]
    rows = out_ref.shape[1]
    x, offset, tokens = place_ref[0], place_ref[1], TOKENS
    start = x * keys
    each = rows - tokens
    wide = GROUP * HD

    def put(place, part, size, out, log):
        out = out.astype(jnp.bfloat16)
        for h in range(GROUP):
            out_ref[place, part, h * HD : (h + 1) * HD] = out[h * size : (h + 1) * size]
        out_ref[place, part, wide:] = stamp([log[h * size : (h + 1) * size] for h in range(GROUP)])

    names = []
    asked = []
    for ref in (q0_ref, q1_ref, q2_ref, q3_ref):
        asked.append(by_head(ref[tokens:rows, :]))
        names.extend([ref[rows:, :HD].astype(jnp.float32)] * (GROUP * each // 16))
    name = jnp.concatenate(names, axis=0)
    low = jnp.zeros(name.shape, jnp.int32)
    high = low
    for b in range(prompts):
        low = jnp.where(name == b, bound_ref[b], low)
        high = jnp.where(name == b, bound_ref[b + 1], high)
    low, high = low[:, :1], high[:, :1]
    pos = start + lax.broadcasted_iota(jnp.int32, (low.shape[0], keys), 1)
    out, log = fold(
        jnp.concatenate(asked, axis=0),
        kv_ref[:, :HD],
        kv_ref[:, HD:],
        (pos >= low) & (pos < high),
    )
    span = GROUP * each
    for k in range(SIDE):
        part = slice(k * span, (k + 1) * span)
        put(lax.rem(x + k, SIDE), slice(tokens, rows), each, out[part], log[part])

    for k, ref in enumerate((q0_ref, q1_ref, q2_ref, q3_ref)):
        asked_ref[k] = by_head(ref[:tokens, :])
    count = tokens * GROUP
    half = keys // 2

    def visit(k, begin, size, masked):
        place = lax.rem(x + k, SIDE)
        visible = None
        if masked:
            token = place * keys + offset
            token = token + lax.rem(lax.broadcasted_iota(jnp.int32, (count, 1), 0), tokens)
            low = jnp.zeros((count, 1), jnp.int32)
            for b in range(1, prompts):
                low = jnp.where(token >= bound_ref[b], bound_ref[b], low)
            pos = start + begin + lax.broadcasted_iota(jnp.int32, (count, size), 1)
            visible = (pos >= low) & (pos <= token)
        part = slice(begin, begin + size)
        out, log = fold(asked_ref[k], kv_ref[part, :HD], kv_ref[part, HD:], visible)
        put(place, slice(0, tokens), tokens, out, log)

    def block(k, carry):
        place = lax.rem(x + k, SIDE)
        first = place * keys + offset
        last = first + tokens - 1
        first_low = jnp.int32(0)
        last_low = jnp.int32(0)
        for b in range(1, prompts):
            first_low = jnp.where(first >= bound_ref[b], bound_ref[b], first_low)
            last_low = jnp.where(last >= bound_ref[b], bound_ref[b], last_low)
        one = (start + half > first_low) & (start <= last)
        two = (start + keys > first_low) & (start + half <= last)
        full = (start >= last_low) & (start + keys <= first + 1)

        @pl.when(jnp.logical_not(one | two))
        def _():
            out_ref[place, :tokens, :wide] = jnp.zeros((tokens, wide), jnp.bfloat16)
            empty = jnp.full((tokens, 1), MASKED, jnp.float32)
            out_ref[place, :tokens, wide:] = stamp([empty] * GROUP)

        @pl.when(full)
        def _():
            visit(k, 0, keys, False)

        @pl.when(one & two & jnp.logical_not(full))
        def _():
            visit(k, 0, keys, True)

        @pl.when(one & jnp.logical_not(two))
        def _():
            visit(k, 0, half, True)

        @pl.when(two & jnp.logical_not(one))
        def _():
            visit(k, half, half, True)

        return carry

    lax.fori_loop(0, SIDE, block, 0)


def merge_kernel(part_ref, own_ref, own_log_ref, out_ref):
    parts, rows, wide = part_ref.shape
    wide = wide - HD
    tokens = TOKENS
    each = rows - tokens

    def merge(part, own):
        lane = lax.broadcasted_iota(jnp.int32, (part.stop - part.start, HD), 1)
        tiles = [part_ref[i, part, wide:].astype(jnp.float32) for i in range(parts)]
        for h in range(GROUP):
            columns = slice(h * HD, (h + 1) * HD)
            mine = (lane >= 3 * h) & (lane < 3 * h + 3)
            logs = [jnp.sum(jnp.where(mine, t, 0.0), axis=1, keepdims=True) for t in tiles]
            outs = [part_ref[i, part, columns].astype(jnp.float32) for i in range(parts)]
            if own:
                some = slice(h * each, (h + 1) * each)
                logs.append(own_log_ref[some, :])
                outs.append(own_ref[some, :])
            top = functools.reduce(jnp.maximum, logs)
            shares = [jnp.exp2(log - top) for log in logs]
            total = functools.reduce(jnp.add, shares)
            done = functools.reduce(jnp.add, [o * w for o, w in zip(outs, shares)]) / total
            done = done.astype(jnp.bfloat16)
            for copy in range(out_ref.shape[0]):
                out_ref[copy, part, columns] = done

    merge(slice(0, tokens), False)
    merge(slice(tokens, rows), True)


def body(
    pre_query,
    pre_key,
    pre_value,
    prompt_lengths,
    out_weight,
    dec_query,
    dec_key,
    dec_value,
    cache_key,
    cache_value,
    cache_lengths,
    row_prompt,
):
    tokens = pre_query.shape[0]
    steps, rows, width = dec_query.shape
    slots = cache_key.shape[1]
    H, L = lax.axis_size("zh"), lax.axis_size("zl")
    x, y, zh, core = (lax.axis_index(a) for a in ("x", "y", "zh", "core"))
    smem = pl.BlockSpec(memory_space=pltpu.SMEM)
    vmem = pl.BlockSpec(memory_space=pltpu.VMEM)
    params = pltpu.CompilerParams(vmem_limit_bytes=40 * 2**20)

    def spread(v, axis):
        return lax.all_to_all(jnp.broadcast_to(v[None], (SIDE,) + v.shape), axis, 0, 0)

    def around(v, axis):
        near = [v]
        for k in range(1, SIDE):
            near.append(lax.ppermute(v, axis, [(i, (i - k) % SIDE) for i in range(SIDE)]))
        return near

    with jax.named_scope("gather_near"):
        kv = jnp.concatenate([pre_key, pre_value], axis=1)
        mid = tokens // 2
        kv = jnp.concatenate([kv[:mid], kv[mid:]], axis=1)
        packed = jnp.concatenate([kv, out_weight.T], axis=0)
        packed = lax.all_gather(packed, "zh", axis=0)
    with jax.named_scope("gather_kv"):
        kv = packed[:, :mid]
        kv = jnp.concatenate([kv[..., : 2 * HD], kv[..., 2 * HD :]], axis=1)
        kv = jnp.broadcast_to(kv[None], (SIDE,) + kv.shape)
        dq = dec_query.reshape(steps * rows, width)
        names = jnp.concatenate([row_prompt, row_prompt]).astype(jnp.bfloat16)
        query = jnp.concatenate(
            [pre_query, dq, jnp.broadcast_to(names[:, None], (2 * rows, width))], axis=0
        )
        query, kv = lax.optimization_barrier((query, kv))
        kv = lax.all_to_all(kv, "y", 0, 0).reshape(-1, 2 * HD)
    with jax.named_scope("gather_query"):
        queries = around(query, "x")
    with jax.named_scope("gather_weight"):
        weight, kv, queries = lax.optimization_barrier((packed[:, mid:], kv, queries))
        weight = spread(weight, "x")

    lanes = steps * rows * GROUP
    with jax.named_scope("cache"):
        own = pl.pallas_call(
            cache_kernel,
            out_shape=(
                jax.ShapeDtypeStruct((lanes, HD), jnp.float32),
                jax.ShapeDtypeStruct((lanes, 1), jnp.float32),
            ),
            in_specs=[smem] + [vmem] * 5,
            out_specs=(vmem, vmem),
            compiler_params=params,
            cost_estimate=pl.CostEstimate(
                flops=4 * lanes * HD * rows * slots,
                bytes_accessed=4 * rows * slots * HD,
                transcendentals=lanes * rows * slots,
            ),
        )(
            cache_lengths,
            dq,
            dec_key.reshape(steps * rows, HD),
            dec_value.reshape(steps * rows, HD),
            cache_key.reshape(rows * slots, HD),
            cache_value.reshape(rows * slots, HD),
        )

    bounds = jnp.concatenate([jnp.zeros((1,), jnp.int32), jnp.cumsum(prompt_lengths)]).astype(
        jnp.int32
    )
    place = jnp.stack([x, (y * H + zh) * tokens]).astype(jnp.int32)
    total = tokens + steps * rows
    count = SIDE * total * GROUP
    with jax.named_scope("attend"):
        parts = pl.pallas_call(
            prompt_kernel,
            out_shape=jax.ShapeDtypeStruct((SIDE, total, width + HD), jnp.bfloat16),
            in_specs=[smem] * 2 + [vmem] * 5,
            out_specs=vmem,
            scratch_shapes=[pltpu.VMEM((SIDE, tokens * GROUP, HD), jnp.bfloat16)],
            compiler_params=params,
            cost_estimate=pl.CostEstimate(
                flops=4 * count * HD * kv.shape[0],
                bytes_accessed=2 * kv.size,
                transcendentals=count * kv.shape[0],
            ),
        )(bounds, place, *queries, kv)
    with jax.named_scope("merge"):
        weight, parts = lax.optimization_barrier((weight, parts))
        weight = weight.reshape(SIDE, 2, -1, width)
        parts = lax.all_to_all(parts, "x", 0, 0)
        attn = pl.pallas_call(
            merge_kernel,
            out_shape=jax.ShapeDtypeStruct((SIDE, total, width), jnp.bfloat16),
            in_specs=[vmem] * 3,
            out_specs=vmem,
            compiler_params=params,
            cost_estimate=pl.CostEstimate(
                flops=8 * parts.size, bytes_accessed=4 * parts.size, transcendentals=parts.size // HD
            ),
        )(parts, *own)

    with jax.named_scope("gather_attn"):
        attn = lax.all_to_all(attn, "y", 0, 0).reshape(SIDE * total, width)
    with jax.named_scope("project"):
        def product(which):
            part = lax.dynamic_index_in_dim(weight, which, 1, keepdims=False)
            return lax.dot_general(
                attn,
                part.reshape(-1, width),
                (((1,), (1,)), ((), ())),
                preferred_element_type=jnp.float32,
            ).astype(jnp.bfloat16)

        swap = [(0, 1), (1, 0)]
        other = lax.ppermute(product(1 - core), "core", swap)
        mine = product(core)
        mine = (mine.astype(jnp.float32) + other.astype(jnp.float32)).astype(jnp.bfloat16)
    with jax.named_scope("scatter"):
        pieces = mine.reshape(SIDE, total, L, HD).transpose(0, 2, 1, 3)
        pieces = lax.all_to_all(pieces.reshape(SIDE * L, total, HD), ("y", "zl"), 0, 0)
        pieces = pieces.reshape(2, 2, L, total, HD)
        pieces = jnp.sum(pieces.astype(jnp.float32), axis=2).astype(jnp.bfloat16)
        keep = lax.dynamic_index_in_dim(pieces, core, 0, keepdims=False)
        give = lax.dynamic_index_in_dim(pieces, 1 - core, 0, keepdims=False)
        take = lax.ppermute(give, "core", swap)
        low = jnp.where(core == 0, keep, take)
        high = jnp.where(core == 0, take, keep)
        result = jnp.concatenate([low[0], high[0], low[1], high[1]], axis=-1)
    return result[:tokens], result[tokens:].reshape(steps, rows, result.shape[1])


def solution(mesh):
    fine = Mesh(mesh.devices.reshape(4, 4, 4, 4, 2), ("x", "y", "zh", "zl", "core"))
    seq, tensor = ("x", "y", "zh"), ("zl", "core")
    placed = (
        P(seq, tensor),
        P(seq, tensor),
        P(seq, tensor),
        P(),
        P(tensor, seq),
        P(None, seq, tensor),
        P(None, seq, tensor),
        P(None, seq, tensor),
        P(seq, None, tensor),
        P(seq, None, tensor),
        P(seq),
        P(seq),
    )
    return jax.shard_map(
        body,
        mesh=fine,
        in_specs=placed,
        out_specs=(P(seq, tensor), P(None, seq, tensor)),
        check_vma=False,
    )
```

time: 156 us -> 139 us (0.89)
  waiting for transfers between devices: 40.7 us -> 22 us
  starting transfers between devices: 47 us -> 37 us
  blocking collectives: 47.6 us -> 54.9 us
  Pallas kernels: 9.28 us -> 15.2 us
    all_to_all x3 -> x4, waiting for transfers between devices: 30.7 us -> 14.2 us  [the longest x1 7.51 us: body(): attn = lax.all_to_all(attn, 'y', 0, 0).reshape(SIDE * total, width)]
    ppermute x3, starting transfers between devices: 16.2 us -> 9.32 us  [around(): lax.ppermute(v, axis, [(i, (i - k) % SIDE) for i in range(SIDE)])]
    pallas_call x2 -> x3, Pallas kernels: 9.28 us -> 15.2 us  [the longest x1 12.1 us: body(): pl.pallas_call(prompt_kernel, out_shape=jax.ShapeDtypeStruct((SIDE, total...]
    all_gather x1, blocking collectives: 25.3 us -> 31.2 us  [body(): packed = lax.all_gather(packed, 'zh', axis=0)]
    all_to_all x3 -> x4, starting transfers between devices: 18.3 us -> 16.1 us  [the longest x1 4.57 us: spread(): lax.all_to_all(jnp.broadcast_to(v[None], (SIDE,) + v.shape), axis, 0, 0)]
    ppermute x3, waiting for transfers between devices: 7.44 us -> 5.19 us  [around(): lax.ppermute(v, axis, [(i, (i - k) % SIDE) for i in range(SIDE)])]
    broadcast_in_dim x3 -> x2, local copies, waits for them, and re-layouts: 4.37 us -> 2.21 us  [the longest x1 1.11 us: body(): kv = jnp.broadcast_to(kv[None], (SIDE,) + kv.shape)]
  transfers between devices with their start and end apart: 8 -> 9, of which waited for: 7 -> 6; matrix products, arithmetic and copies ran while one was open for 0% -> 0% of each run, Pallas kernels for 6% -> 10%
where the time goes in v3:
time: 139 us; the launch traced here: 138 us
  blocking collectives  54.9 us (39%)
  starting transfers between devices  37 us (27%)
  waiting for transfers between devices  22 us (16%)
  Pallas kernels  15.2 us (11%)
  local copies, waits for them, and re-layouts  4.86 us (3%)
  other arithmetic  2.15 us (2%)
    all_gather x1, blocking collectives, body(): packed = lax.all_gather(packed, 'zh', axis=0)  31.2 us
    all_to_all x1, blocking collectives, body(): lax.all_to_all(pieces.reshape(SIDE * L, total, HD), ('y', 'zl'), 0, 0)  23.7 us
    pallas_call x1, Pallas kernels, body(): pl.pallas_call(prompt_kernel, out_shape=jax.ShapeDtypeStruct((SIDE, total...  12.1 us
    ppermute x3, starting transfers between devices, around(): lax.ppermute(v, axis, [(i, (i - k) % SIDE) for i in range(SIDE)])  9.32 us
    ppermute x1, starting transfers between devices, body(): other = lax.ppermute(product(1 - core), 'core', swap)  8.34 us
    all_to_all x1, waiting for transfers between devices, body(): attn = lax.all_to_all(attn, 'y', 0, 0).reshape(SIDE * total, width)  7.51 us
    all_to_all x1, waiting for transfers between devices, body(): parts = lax.all_to_all(parts, 'x', 0, 0)  6.72 us
    ppermute x3, waiting for transfers between devices, around(): lax.ppermute(v, axis, [(i, (i - k) % SIDE) for i in range(SIDE)])  5.19 us
  transfers between devices with their start and end apart: 9, of which 6 were waited for; matrix products, arithmetic and copies ran while one was open for 0% of the time, Pallas kernels for 10%

profile of v3, /device:TPU:1, one launch (start us, length us, event | category | flops | bytes accessed | tf_op | source)
XLA Modules:
  0.0 138.2 jit_solution(6933728278244565321)
XLA Ops:
  0.6 0.8 constant_dynamic-update-slice_fusion.1
  1.4 0.8 constant_dynamic-update-slice_fusion
  2.2 0.9 pad_maximum_fusion.2
  3.1 31.2 %all-gather = bf16[512,512]{1,0:T(8,128)(2,1)S(1)} all-gather(bf16[128,512]{1,0:T(8,128)(2,1)S(1)} %pad_maximum_fusion.2), channel_id=2, replica_groups=mesh['x'=4,'y'=4,'zh'=4,'zl'=4,'core'=2] {'zh'}, dimensions={0}, use_global_device_ids=true | all-gather | bytes 655360 | tf_op jit(solution)/shard_map/gather_near/all_gather | solution.py:241
  34.6 1.1 broadcast_in_dim.7
  35.7 4.2 %all-to-all-start = ((bf16[4,4,128,256]{3,2,1,0:T(8,128)(2,1)}), bf16[4,4,128,256]{3,2,1,0:T(8,128)(2,1)S(1)}, u32[]{:S(2)}, u32[]{:S(2)}) async-start(bf16[4,4,128,256]{3,2,1,0:T(8,128)(2,1)} %broadcast_in_dim.7), calls=%async_computation | async-start | bytes 2097152 | tf_op jit(solution)/shard_map/gather_kv/all_to_all | solution.py:252
  39.9 4.4 %collective-permute-start = (bf16[176,512]{1,0:T(8,128)(2,1)S(1)}, bf16[176,512]{1,0:T(8,128)(2,1)S(1)}, u32[]{:S(2)}, u32[]{:S(2)}) collective-permute-start(bf16[176,512]{1,0:T(8,128)(2,1)S(1)} %maximum_maximum_fusion.q0_ref), channel_id=1, source_target_pairs={{0,384},{128,0},{256,128},{384,256},{1,385},{129,1},{257,129},{385... | collective-permute-start | bytes 540680 | tf_op jit(solution)/shard_map/gather_query/ppermute | solution.py:233
  44.2 2.4 %collective-permute-start.1 = (bf16[176,512]{1,0:T(8,128)(2,1)S(1)}, bf16[176,512]{1,0:T(8,128)(2,1)S(1)}, u32[]{:S(2)}, u32[]{:S(2)}) collective-permute-start(bf16[176,512]{1,0:T(8,128)(2,1)S(1)} %maximum_maximum_fusion.q0_ref), channel_id=1, source_target_pairs={{0,256},{128,384},{256,0},{384,128},{1,257},{129,385},{257,1},{385... | collective-permute-start | bytes 540680 | tf_op jit(solution)/shard_map/gather_query/ppermute | solution.py:233
  46.7 2.5 %collective-permute-start.2 = (bf16[176,512]{1,0:T(8,128)(2,1)S(1)}, bf16[176,512]{1,0:T(8,128)(2,1)S(1)}, u32[]{:S(2)}, u32[]{:S(2)}) collective-permute-start(bf16[176,512]{1,0:T(8,128)(2,1)S(1)} %maximum_maximum_fusion.q0_ref), channel_id=1, source_target_pairs={{0,128},{128,256},{256,384},{384,0},{1,129},{129,257},{257,385},{3... | collective-permute-start | bytes 540680 | tf_op jit(solution)/shard_map/gather_query/ppermute | solution.py:233
  49.2 2.7 %collective-permute-done.1.q2_ref = bf16[176,512]{1,0:T(8,128)(2,1)S(1)} collective-permute-done((bf16[176,512]{1,0:T(8,128)(2,1)S(1)}, bf16[176,512]{1,0:T(8,128)(2,1)S(1)}, u32[]{:S(2)}, u32[]{:S(2)}) %collective-permute-start.1) | collective-permute-done | bytes 180256 | tf_op jit(solution)/shard_map/gather_query/ppermute | solution.py:233
  52.0 2.4 %collective-permute-done.2.q3_ref = bf16[176,512]{1,0:T(8,128)(2,1)S(1)} collective-permute-done((bf16[176,512]{1,0:T(8,128)(2,1)S(1)}, bf16[176,512]{1,0:T(8,128)(2,1)S(1)}, u32[]{:S(2)}, u32[]{:S(2)}) %collective-permute-start.2) | collective-permute-done | bytes 180256 | tf_op jit(solution)/shard_map/gather_query/ppermute | solution.py:233
  54.4 1.1 broadcast_in_dim.8
  55.5 4.6 %all-to-all-start.1 = ((bf16[4,4,64,512]{3,2,1,0:T(8,128)(2,1)}), bf16[4,4,64,512]{3,2,1,0:T(8,128)(2,1)S(1)}, u32[]{:S(2)}, u32[]{:S(2)}) async-start(bf16[4,4,64,512]{3,2,1,0:T(8,128)(2,1)} %broadcast_in_dim.8), calls=%async_computation.1 | async-start | bytes 2097152 | tf_op jit(solution)/shard_map/gather_weight/all_to_all | solution.py:228
  60.1 0.2 reduce-window.9
  60.4 12.1 %attend.1 = bf16[4,160,640]{2,1,0:T(8,128)(2,1)} custom-call(s32[5]{0:T(128)S(1)} %pad_add_fusion.bound_ref, s32[2]{0:T(128)S(1)} %pad_add_fusion.1.place_ref, bf16[176,512]{1,0:T(8,128)(2,1)S(1)} %maximum_maximum_fusion.q0_ref, bf16[176,512]{1,0:T(8,128)(2,1)S(1)} %collective-permute-done.q1_ref, bf16[176,512]{1,0:T(8,128)(2,1)S(1)} %collective-permute-done.1.q2_ref, ...), custom_call_target="tpu_custom_call" | custom-call | flops 2684354560 | bytes 1048576 | tf_op jit(solution)/shard_map/attend/pallas_call | solution.py:291
  72.6 3.8 %all-to-all-start.2 = ((bf16[4,160,640]{2,1,0:T(8,128)(2,1)}), bf16[4,160,640]{2,1,0:T(8,128)(2,1)S(1)}, u32[]{:S(2)}, u32[]{:S(2)}) async-start(bf16[4,160,640]{2,1,0:T(8,128)(2,1)} %attend.1), calls=%async_computation.2 | async-start | bytes 1638400 | tf_op jit(solution)/shard_map/merge/all_to_all | solution.py:307
  76.5 1.6 %cache.1 = (f32[128,128]{1,0:T(8,128)S(1)}, f32[128,1]{1,0:T(8,128)S(1)}) custom-call(s32[8]{0:T(128)S(1)} %copy-done.5, bf16[32,512]{1,0:T(8,128)(2,1)S(1)} %bitcast.44, bf16[32,128]{1,0:T(8,128)(2,1)S(1)} %bitcast.45, bf16[32,128]{1,0:T(8,128)(2,1)S(1)} %bitcast.46, bf16[2048,128]{1,0:T(8,128)(2,1)S(1)} %bitcast.41, bf16[2048,128]{1,0:T(8,128)(2,1)S(1)} %bitcast.42), custom_call_target="tpu_custom_call" | custom-call | flops 134217728 | bytes 1048576 | tf_op jit(solution)/shard_map/cache/pallas_call | solution.py:261
  78.0 6.7 %all-to-all-done.2.part_ref = bf16[4,160,640]{2,1,0:T(8,128)(2,1)S(1)} async-done(((bf16[4,160,640]{2,1,0:T(8,128)(2,1)}), bf16[4,160,640]{2,1,0:T(8,128)(2,1)S(1)}, u32[]{:S(2)}, u32[]{:S(2)}) %all-to-all-start.2) | async-done | bytes 819232 | tf_op jit(solution)/shard_map/merge/all_to_all | solution.py:307
  84.8 1.5 %merge.1 = bf16[4,160,512]{2,1,0:T(8,128)(2,1)} custom-call(bf16[4,160,640]{2,1,0:T(8,128)(2,1)S(1)} %all-to-all-done.2.part_ref, f32[128,128]{1,0:T(8,128)S(1)} %get-tuple-element.23.own_ref, f32[128,1]{1,0:T(8,128)S(1)} %get-tuple-element.24.own_log_ref), custom_call_target="tpu_custom_call" | custom-call | flops 3276800 | bytes 1638400 | tf_op jit(solution)/shard_map/merge/pallas_call | solution.py:308
  86.3 3.5 %all-to-all-start.3 = ((bf16[4,160,512]{2,1,0:T(8,128)(2,1)}), bf16[4,160,512]{2,1,0:T(8,128)(2,1)S(1)}, u32[]{:S(2)}, u32[]{:S(2)}) async-start(bf16[4,160,512]{2,1,0:T(8,128)(2,1)} %merge.1), calls=%async_computation.3 | async-start | bytes 1310720 | tf_op jit(solution)/shard_map/gather_attn/all_to_all | solution.py:320
  89.9 7.5 %all-to-all-done.3 = bf16[4,160,512]{2,1,0:T(8,128)(2,1)S(1)} async-done(((bf16[4,160,512]{2,1,0:T(8,128)(2,1)}), bf16[4,160,512]{2,1,0:T(8,128)(2,1)S(1)}, u32[]{:S(2)}, u32[]{:S(2)}) %all-to-all-start.3) | async-done | bytes 655392 | tf_op jit(solution)/shard_map/gather_attn/all_to_all | solution.py:320
  97.4 0.5 convolution_convert_fusion
  97.9 8.3 %collective-permute-start.3 = (bf16[640,512]{1,0:T(8,128)(2,1)S(1)}, bf16[640,512]{1,0:T(8,128)(2,1)S(1)}, u32[]{:S(2)}, u32[]{:S(2)}) collective-permute-start(bf16[640,512]{1,0:T(8,128)(2,1)S(1)} %convolution_convert_fusion), channel_id=1, source_target_pairs={{0,1},{1,0},{2,3},{3,2},{4,5},{5,4},{6,7},{7,6},{8,9},{9,8},{10,11... | collective-permute-start | bytes 1966088 | tf_op jit(solution)/shard_map/project/ppermute | solution.py:332
  106.3 1.7 %collective-permute-done.3 = bf16[640,512]{1,0:T(8,128)(2,1)S(1)} collective-permute-done((bf16[640,512]{1,0:T(8,128)(2,1)S(1)}, bf16[640,512]{1,0:T(8,128)(2,1)S(1)}, u32[]{:S(2)}, u32[]{:S(2)}) %collective-permute-start.3) | collective-permute-done | bytes 655392 | tf_op jit(solution)/shard_map/project/ppermute | solution.py:332
  108.0 0.5 add_convert_fusion
  108.5 0.2 reshape.103
  108.7 0.1 copy.14
  108.8 23.7 %all_to_all.25 = bf16[16,160,128]{2,1,0:T(8,128)(2,1)S(1)} all-to-all(bf16[16,160,128]{2,1,0:T(8,128)(2,1)S(1)} %bitcast.48), channel_id=1, replica_groups=mesh['x'=4,'y'=4,'zh'=4,'zl'=4,'core'=2] {'y','zl'}, dimensions={0} | all-to-all | bytes 1310720 | tf_op jit(solution)/shard_map/scatter/all_to_all | solution.py:337
  132.6 3.3 %collective-permute-start.4 = (bf16[2,160,128]{2,1,0:T(8,128)(2,1)S(1)}, bf16[2,160,128]{2,1,0:T(8,128)(2,1)S(1)}, u32[]{:S(2)}, u32[]{:S(2)}) collective-permute-start(bf16[2,160,128]{2,1,0:T(8,128)(2,1)S(1)} %dynamic-slice_bitcast_fusion), channel_id=1, source_target_pairs={{0,1},{1,0},{2,3},{3,2},{4,5},{5,4},{6,7},{7,6},{8,9},{9,8},{10,11... | collective-permute-start | bytes 245768 | tf_op jit(solution)/shard_map/scatter/ppermute | solution.py:342
  135.9 0.9 collective-permute-done.4
  136.9 0.6 maximum_bitcast_fusion
  137.5 0.7 slice.56
  (36 shorter events, 0.7 us)
Async XLA Ops:
  0.6 33.7 %copy-start.7 = (s32[8]{0:T(128)S(1)}, s32[8]{0:T(128)}, u32[]{:S(2)}) copy-start(s32[8]{0:T(128)} %param.23) | copy-start | bytes 100
  2.2 32.3 %copy-start.2 = (bf16[4,8,512]{2,1,0:T(8,128)(2,1)S(1)}, bf16[4,8,512]{2,1,0:T(8,128)(2,1)}, u32[]{:S(2)}) copy-start(bf16[4,8,512]{2,1,0:T(8,128)(2,1)} %param.17) | copy-start | bytes 98308
  2.2 32.3 %copy-start.6 = (bf16[128,512]{1,0:T(8,128)(2,1)S(1)}, bf16[128,512]{1,0:T(8,128)(2,1)}, u32[]{:S(2)}) copy-start(bf16[128,512]{1,0:T(8,128)(2,1)} %param.12) | copy-start | bytes 393220
  35.7 18.8 %all-to-all-start = ((bf16[4,4,128,256]{3,2,1,0:T(8,128)(2,1)}), bf16[4,4,128,256]{3,2,1,0:T(8,128)(2,1)S(1)}, u32[]{:S(2)}, u32[]{:S(2)}) async-start(bf16[4,4,128,256]{3,2,1,0:T(8,128)(2,1)} %broadcast_in_dim.7), calls=%async_computation | async-start | bytes 2097152 | tf_op jit(solution)/shard_map/gather_kv/all_to_all | solution.py:252
  39.9 9.4 %collective-permute-start = (bf16[176,512]{1,0:T(8,128)(2,1)S(1)}, bf16[176,512]{1,0:T(8,128)(2,1)S(1)}, u32[]{:S(2)}, u32[]{:S(2)}) collective-permute-start(bf16[176,512]{1,0:T(8,128)(2,1)S(1)} %maximum_maximum_fusion.q0_ref), channel_id=1, source_target_pairs={{0,384},{128,0},{256,128},{384,256},{1,385},{129,1},{257,129},{385... | collective-permute-start | bytes 540680 | tf_op jit(solution)/shard_map/gather_query/ppermute | solution.py:233
  44.2 7.7 %collective-permute-start.1 = (bf16[176,512]{1,0:T(8,128)(2,1)S(1)}, bf16[176,512]{1,0:T(8,128)(2,1)S(1)}, u32[]{:S(2)}, u32[]{:S(2)}) collective-permute-start(bf16[176,512]{1,0:T(8,128)(2,1)S(1)} %maximum_maximum_fusion.q0_ref), channel_id=1, source_target_pairs={{0,256},{128,384},{256,0},{384,128},{1,257},{129,385},{257,1},{385... | collective-permute-start | bytes 540680 | tf_op jit(solution)/shard_map/gather_query/ppermute | solution.py:233
  46.7 7.7 %collective-permute-start.2 = (bf16[176,512]{1,0:T(8,128)(2,1)S(1)}, bf16[176,512]{1,0:T(8,128)(2,1)S(1)}, u32[]{:S(2)}, u32[]{:S(2)}) collective-permute-start(bf16[176,512]{1,0:T(8,128)(2,1)S(1)} %maximum_maximum_fusion.q0_ref), channel_id=1, source_target_pairs={{0,128},{128,256},{256,384},{384,0},{1,129},{129,257},{257,385},{3... | collective-permute-start | bytes 540680 | tf_op jit(solution)/shard_map/gather_query/ppermute | solution.py:233
  55.5 4.6 %copy-start.8 = (s32[4]{0:T(128)S(1)}, s32[4]{0:T(128)}, u32[]{:S(2)}) copy-start(s32[4]{0:T(128)} %param.15) | copy-start | bytes 52
  55.5 17.1 %all-to-all-start.1 = ((bf16[4,4,64,512]{3,2,1,0:T(8,128)(2,1)}), bf16[4,4,64,512]{3,2,1,0:T(8,128)(2,1)S(1)}, u32[]{:S(2)}, u32[]{:S(2)}) async-start(bf16[4,4,64,512]{3,2,1,0:T(8,128)(2,1)} %broadcast_in_dim.8), calls=%async_computation.1 | async-start | bytes 2097152 | tf_op jit(solution)/shard_map/gather_weight/all_to_all | solution.py:228
  72.6 3.9 %copy-start = (bf16[8,256,128]{2,1,0:T(8,128)(2,1)S(1)}, bf16[8,256,128]{2,1,0:T(8,128)(2,1)}, u32[]{:S(2)}) copy-start(bf16[8,256,128]{2,1,0:T(8,128)(2,1)} %param.20) | copy-start | bytes 1572868
  72.6 3.9 %copy-start.1 = (bf16[8,256,128]{2,1,0:T(8,128)(2,1)S(1)}, bf16[8,256,128]{2,1,0:T(8,128)(2,1)}, u32[]{:S(2)}) copy-start(bf16[8,256,128]{2,1,0:T(8,128)(2,1)} %param.21) | copy-start | bytes 1572868
  72.6 3.9 %copy-start.3 = (bf16[4,8,128]{2,1,0:T(8,128)(2,1)S(1)}, bf16[4,8,128]{2,1,0:T(8,128)(2,1)}, u32[]{:S(2)}) copy-start(bf16[4,8,128]{2,1,0:T(8,128)(2,1)} %param.18) | copy-start | bytes 24580
  72.6 3.9 %copy-start.4 = (bf16[4,8,128]{2,1,0:T(8,128)(2,1)S(1)}, bf16[4,8,128]{2,1,0:T(8,128)(2,1)}, u32[]{:S(2)}) copy-start(bf16[4,8,128]{2,1,0:T(8,128)(2,1)} %param.19) | copy-start | bytes 24580
  72.6 3.9 %copy-start.5 = (s32[8]{0:T(128)S(1)}, s32[8]{0:T(128)}, u32[]{:S(2)}) copy-start(s32[8]{0:T(128)} %len_ref.1) | copy-start | bytes 100
  72.6 12.2 %all-to-all-start.2 = ((bf16[4,160,640]{2,1,0:T(8,128)(2,1)}), bf16[4,160,640]{2,1,0:T(8,128)(2,1)S(1)}, u32[]{:S(2)}, u32[]{:S(2)}) async-start(bf16[4,160,640]{2,1,0:T(8,128)(2,1)} %attend.1), calls=%async_computation.2 | async-start | bytes 1638400 | tf_op jit(solution)/shard_map/merge/all_to_all | solution.py:307
  86.3 11.1 %all-to-all-start.3 = ((bf16[4,160,512]{2,1,0:T(8,128)(2,1)}), bf16[4,160,512]{2,1,0:T(8,128)(2,1)S(1)}, u32[]{:S(2)}, u32[]{:S(2)}) async-start(bf16[4,160,512]{2,1,0:T(8,128)(2,1)} %merge.1), calls=%async_computation.3 | async-start | bytes 1310720 | tf_op jit(solution)/shard_map/gather_attn/all_to_all | solution.py:320
  97.9 10.1 %collective-permute-start.3 = (bf16[640,512]{1,0:T(8,128)(2,1)S(1)}, bf16[640,512]{1,0:T(8,128)(2,1)S(1)}, u32[]{:S(2)}, u32[]{:S(2)}) collective-permute-start(bf16[640,512]{1,0:T(8,128)(2,1)S(1)} %convolution_convert_fusion), channel_id=1, source_target_pairs={{0,1},{1,0},{2,3},{3,2},{4,5},{5,4},{6,7},{7,6},{8,9},{9,8},{10,11... | collective-permute-start | bytes 1966088 | tf_op jit(solution)/shard_map/project/ppermute | solution.py:332
  132.6 4.2 %collective-permute-start.4 = (bf16[2,160,128]{2,1,0:T(8,128)(2,1)S(1)}, bf16[2,160,128]{2,1,0:T(8,128)(2,1)S(1)}, u32[]{:S(2)}, u32[]{:S(2)}) collective-permute-start(bf16[2,160,128]{2,1,0:T(8,128)(2,1)S(1)} %dynamic-slice_bitcast_fusion), channel_id=1, source_target_pairs={{0,1},{1,0},{2,3},{3,2},{4,5},{5,4},{6,7},{7,6},{8,9},{9,8},{10,11... | collective-permute-start | bytes 245768 | tf_op jit(solution)/shard_map/scatter/ppermute | solution.py:342
